TPU v7x, 512 devices: a whole 4x8x8 slice. The times are simulated.
512 devices in a mesh: aa: 32 (over y, x), ba: 16 (over z, core).
Axes of the slice: x: 4, y: 8, z: 8, core: 2. Of those that a mesh axis runs over, the one named last changes fastest.
Arguments:
- feat_a: bfloat16 [16384, 256], P(('aa', 'ba')), may hold values from -32 to 32
- feat_b: bfloat16 [65536, 256], P(('ba', 'aa')), may hold values from -32 to 32
- col_max_other: float32 [65536], P('ba'), may hold values from 1 to 3
- col_sum_other: float32 [65536], P('ba'), may hold values from 5734.4 to 114688
Outputs:
- confidence: bfloat16 [16384, 65536], P('aa', 'ba')
All inputs are finite; a program needn't handle non-finite values.
Results may differ from a plain program's by a relative error of at most 0.0034.
Values may be sent and summed in bfloat16 or wider, within the bound.
No kernel may reach another device: no remote copies, remote signals or barrier semaphores. Data moves between devices by JAX's collectives and lax.ppermute only.
A program may use at most 64 MiB of HBM per device.

v0:
```python
import jax
import jax.numpy as jnp
from jax import lax
from jax.sharding import PartitionSpec as P

FRAME_A = 131072


temper = 0.1


def local_statistics(tile_scores):
    row_top = jnp.max(tile_scores, axis=1)
    row_tot = jnp.sum(jnp.exp(tile_scores - row_top[:, None]), axis=1)
    col_top = jnp.max(tile_scores, axis=0)
    col_tot = jnp.sum(jnp.exp(tile_scores - col_top[None, :]), axis=0)
    return (row_top, row_tot, col_top, col_tot)


def finish(tile_scores, row_max, row_sum, col_max, col_sum, scale_up):
    row_part = jnp.exp(tile_scores - row_max[:, None]) / row_sum[:, None]
    col_part = jnp.exp(tile_scores - col_max[None, :]) / col_sum[None, :]
    return (row_part * col_part * scale_up).astype(jnp.bfloat16)


def local(feat_a, feat_b, col_max_other, col_sum_other):
    slab_feats = lax.all_gather(feat_a, "ba", axis=0, tiled=True)
    factor = 1.0 / (feat_a.shape[1] * temper)
    columns = feat_b.shape[0] * lax.axis_size("aa")
    scale_up = float(FRAME_A) * float(columns * lax.axis_size("ba"))
    kept_scores = (
        jnp.dot(
            slab_feats,
            lax.all_gather(feat_b, "aa", axis=0, tiled=True).T,
            preferred_element_type=jnp.float32,
        )
        * factor
    )
    row_top, row_tot, col_top, col_tot = local_statistics(kept_scores)
    row_max = lax.pmax(row_top, "ba")
    row_sum = lax.psum(row_tot * jnp.exp(row_top - row_max), "ba")
    slab_max = lax.pmax(col_top, "aa")
    col_max = jnp.maximum(slab_max, col_max_other)
    col_sum = lax.psum(col_tot * jnp.exp(col_top - col_max), "aa")
    col_sum = col_sum + col_sum_other * jnp.exp(col_max_other - col_max)
    return finish(kept_scores, row_max, row_sum, col_max, col_sum, scale_up)


def solution(mesh):
    in_specs = (P(("aa", "ba"), None), P(("ba", "aa"), None), P("ba"), P("ba"))
    out_specs = P("aa", "ba")
    return jax.shard_map(local, mesh=mesh, in_specs=in_specs, out_specs=out_specs, check_vma=False)
```

profile of v0, /device:TPU:32, one launch (start us, length us, event | category | flops | bytes accessed | tf_op | source)
XLA Modules:
  0.0 449.3 jit_solution(10774058771759965392)
XLA Ops:
  6.5 0.0 all-gather.2.cloned.1.call-start
  6.5 0.7 all-gather.2.cloned.1.call-update
  7.3 24.1 %all_gather.6 = bf16[512,256]{1,0:T(8,128)(2,1)S(1)} all-gather(bf16[32,256]{1,0:T(8,128)(2,1)} %param.4), channel_id=1, replica_groups=mesh['aa'=32,'ba'=16] {'ba'}, dimensions={0}, use_global_device_ids=true | all-gather | bytes 278528 | tf_op jit(solution)/shard_map/all_gather | solution.py:27
  31.4 64.2 %all-gather.2.cloned.1.call-done = bf16[4096,256]{1,0:T(8,128)(2,1)} async-done(((bf16[128,256]{1,0:T(8,128)(2,1)}), bf16[4096,256]{1,0:T(8,128)(2,1)}) %all-gather.2.cloned.1.call-update) | async-done | bytes 2097168 | tf_op jit(solution)/shard_map/all_gather | solution.py:34
  95.6 6.1 %fusion = (f32[512]{0:T(512)S(1)}, f32[512,4096]{1,0:T(8,128)}) fusion(bf16[512,256]{1,0:T(8,128)(2,1)S(1)} %all_gather.6, bf16[4096,256]{1,0:T(8,128)(2,1)} %all-gather.2.cloned.1.call-done), kind=kOutput, calls=%fused_computation.7 | convolution fusion | flops 1077935616 | bytes 10749952 | tf_op jit(solution)/shard_map/dot_general | solution.py:32
  101.7 24.2 %pmax.14 = f32[512]{0:T(512)S(1)} all-reduce(f32[512]{0:T(512)S(1)} %get-tuple-element.9), channel_id=1, replica_groups=mesh['aa'=32,'ba'=16] {'ba'}, use_global_device_ids=true, to_apply=%region_1.0 | all-reduce | flops 512 | bytes 4096 | tf_op jit(solution)/shard_map/pmax | solution.py:40
  125.8 0.0 copy-start
  125.8 0.0 copy-start.1
  125.9 0.0 copy-start.2
  125.9 4.8 %exponential_reduce_fusion.1 = (f32[512]{0:T(512)S(1)}, f32[4096]{0:T(1024)S(1)}) fusion(f32[512,4096]{1,0:T(8,128)} %get-tuple-element.10, f32[512]{0:T(512)S(1)} %get-tuple-element.9), kind=kLoop, calls=%fused_computation.2 | loop fusion | flops 6286848 | bytes 8409088 | tf_op jit(solution)/shard_map/reduce_sum | solution.py:14
  130.6 1.1 copy-done
  131.7 1.3 exponential_reduce_fusion
  133.0 141.1 %pmax.15 = f32[4096]{0:T(1024)S(1)} all-reduce(f32[4096]{0:T(1024)S(1)} %get-tuple-element.6), channel_id=1, replica_groups=mesh['aa'=32,'ba'=16] {'aa'}, use_global_device_ids=true, to_apply=%region_5.0 | all-reduce | flops 4096 | bytes 32768 | tf_op jit(solution)/shard_map/pmax | solution.py:42
  274.1 23.5 %psum.14 = f32[512]{0:T(512)S(1)} all-reduce(f32[512]{0:T(512)S(1)} %exponential_multiply_fusion.1), channel_id=1, replica_groups=mesh['aa'=32,'ba'=16] {'ba'}, use_global_device_ids=true, to_apply=%region_3.0 | all-reduce | flops 512 | bytes 4096 | tf_op jit(solution)/shard_map/psum | solution.py:41
  297.6 0.0 copy-done.1
  297.6 137.7 %psum.15 = f32[4096]{0:T(1024)S(1)} all-reduce(f32[4096]{0:T(1024)S(1)} %get-tuple-element.7), channel_id=1, replica_groups=mesh['aa'=32,'ba'=16] {'aa'}, use_global_device_ids=true, to_apply=%region_7.0 | all-reduce | flops 4096 | bytes 32768 | tf_op jit(solution)/shard_map/psum | solution.py:44
  435.4 0.0 copy-done.2
  435.4 7.1 %multiply_convert_fusion = bf16[512,4096]{1,0:T(8,128)(2,1)} fusion(f32[512,4096]{1,0:T(8,128)} %get-tuple-element.10, f32[4096]{0:T(1024)S(1)} %multiply_add_fusion, f32[4096]{0:T(1024)S(1)} %get-tuple-element.8, f32[512]{0:T(512)S(1)} %psum.14, f32[512]{0:T(512)S(1)} %pmax.14), kind=kLoop, calls=%fused_computation | loop fusion | flops 14680064 | bytes 12619776 | tf_op jit(solution)/shard_map/convert_element_type | solution.py:23
  (3 shorter events, 0.0 us)
Async XLA Ops:
  6.5 89.0 %all-gather.2.cloned.1.call-start = ((), (), s32[]{:S(2)}) async-start(), calls=%async_computation | async-start | bytes 2162688 | tf_op jit(solution)/shard_map/all_gather | solution.py:34
  125.8 5.8 %copy-start = (f32[512,4096]{1,0:T(8,128)S(1)}, f32[512,4096]{1,0:T(8,128)}, u32[]{:S(2)}) copy-start(f32[512,4096]{1,0:T(8,128)} %get-tuple-element.10) | copy-start | bytes 25165828
  125.8 171.8 %copy-start.1 = (f32[4096]{0:T(1024)S(1)}, f32[4096]{0:T(1024)}, u32[]{:S(2)}) copy-start(f32[4096]{0:T(1024)} %param.6) | copy-start | bytes 49156
  125.9 309.5 %copy-start.2 = (f32[4096]{0:T(1024)S(1)}, f32[4096]{0:T(1024)}, u32[]{:S(2)}) copy-start(f32[4096]{0:T(1024)} %param.7) | copy-start | bytes 49156
Sparse Core Ops, SparseCore 0:
  10.5 85.0 all-gather.1
where the time goes:
time: 450 us; the launch traced here: 449 us
  blocking collectives  351 us (78%)
  waiting for transfers between devices  64.9 us (14%)
  between operations  13.4 us (3%)
  other arithmetic  13.2 us (3%)
  matrix products  6.1 us (1%)
    pmax x1, blocking collectives, local(): slab_max = lax.pmax(col_top, 'aa')  141 us
    psum x1, blocking collectives, local(): col_sum = lax.psum(col_tot * jnp.exp(col_top - col_max), 'aa')  138 us
    all_gather x1, waiting for transfers between devices, local(): lax.all_gather(feat_b, 'aa', axis=0, tiled=True)  64.2 us
    pmax x1, blocking collectives, local(): row_max = lax.pmax(row_top, 'ba')  24.2 us
    all_gather x1, blocking collectives, local(): slab_feats = lax.all_gather(feat_a, 'ba', axis=0, tiled=True)  24.1 us
    psum x1, blocking collectives, local(): row_sum = lax.psum(row_tot * jnp.exp(row_top - row_max), 'ba')  23.5 us
  transfers between devices with their start and end apart: 1, of which 1 were waited for; matrix products, arithmetic and copies ran while one was open for 0% of the time, Pallas kernels for 0%

commit v1 on v0

v1 whole, which is shorter than its diff:
```python
import functools
import math

import jax
import jax.numpy as jnp
from jax import lax
from jax.experimental import pallas as pl
from jax.experimental.pallas import tpu as pltpu
from jax.sharding import Mesh
from jax.sharding import PartitionSpec as P

FRAME_A = 131072
TEMPER = 0.1
LOG2E = math.log2(math.e)
AA = ("y", "x")
BA = ("z", "core")


def spread(block, axis):
    n = lax.axis_size(axis)
    return lax.all_to_all(jnp.broadcast_to(block[None], (n,) + block.shape), axis, 0, 0, tiled=True)


def block_scores(a_ref, b_ref, j, factor):
    b = b_ref[:, j].reshape(-1, b_ref.shape[-1])
    d = lax.dot_general(a_ref[...], b, (((1,), (1,)), ((), ())), preferred_element_type=jnp.float32)
    return d * (factor * LOG2E)


def stats_kernel(factor, a_ref, b_ref, row_ref, col_ref, s_ref):
    rows, columns = a_ref.shape[0], col_ref.shape[1]
    blocks = b_ref.shape[1]
    width = columns // blocks
    lanes = 128

    def first(j, top):
        s = block_scores(a_ref, b_ref, j, factor)
        at = pl.ds(pl.multiple_of(j * width, width), width)
        s_ref[:, at] = s
        col_top = jnp.max(s, axis=0, keepdims=True)
        col_tot = jnp.sum(jnp.exp2(s - col_top), axis=0, keepdims=True)
        col_ref[:, at] = col_top + jnp.log2(col_tot)
        for c in range(0, width, lanes):
            top = jnp.maximum(top, s[:, c : c + lanes])
        return top

    top = lax.fori_loop(0, blocks, first, jnp.full((rows, lanes), -jnp.inf, jnp.float32))
    row_top = jnp.max(top, axis=1, keepdims=True)

    def second(j, tot):
        at = pl.ds(pl.multiple_of(j * width, width), width)
        e = jnp.exp2(s_ref[:, at] - row_top)
        for c in range(0, width, lanes):
            tot = tot + e[:, c : c + lanes]
        return tot

    tot = lax.fori_loop(0, blocks, second, jnp.zeros((rows, lanes), jnp.float32))
    lse = row_top + jnp.log2(jnp.sum(tot, axis=1, keepdims=True))
    row_ref[...] = jnp.broadcast_to(lse, (rows, lanes)).T[:1]


def stats(a, b, factor):
    rows = a.shape[0]
    columns = b.shape[0] * b.shape[1] * b.shape[2]
    vmem = pl.BlockSpec(memory_space=pltpu.VMEM)
    return pl.pallas_call(
        functools.partial(stats_kernel, factor),
        out_shape=(
            jax.ShapeDtypeStruct((1, rows), jnp.float32),
            jax.ShapeDtypeStruct((1, columns), jnp.float32),
        ),
        in_specs=[vmem, vmem],
        out_specs=(vmem, vmem),
        scratch_shapes=[pltpu.VMEM((rows, columns), jnp.float32)],
        compiler_params=pltpu.CompilerParams(vmem_limit_bytes=40 << 20),
        name="tile_statistics",
    )(a, b)


def finish_kernel(factor, shift, a_ref, b_ref, rows_ref, cols_ref, top_ref, tot_ref, out_ref, row_lse):
    j = pl.program_id(0)

    @pl.when(j == 0)
    def _():
        parts = rows_ref[:, 0]
        top = jnp.max(parts, axis=0, keepdims=True)
        lse = top + jnp.log2(jnp.sum(jnp.exp2(parts - top), axis=0, keepdims=True))
        row_lse[...] = jnp.broadcast_to(lse, (128, lse.shape[1])).T

    parts = cols_ref[:, 0]
    other_top = top_ref[...] * LOG2E
    top = jnp.maximum(jnp.max(parts, axis=0, keepdims=True), other_top)
    tot = jnp.sum(jnp.exp2(parts - top), axis=0, keepdims=True) + tot_ref[...] * jnp.exp2(other_top - top)
    col_lse = top + jnp.log2(tot) - shift
    s = block_scores(a_ref, b_ref, 0, factor)
    out_ref[...] = jnp.exp2((s - row_lse[:, :1]) + (s - col_lse)).astype(out_ref.dtype)


def finish(a, b, row_parts, col_parts, col_max_other, col_sum_other, factor, shift):
    rows = a.shape[0]
    nx, ny, n, c = b.shape
    columns = nx * ny * n
    width = nx * n
    na, nb = col_parts.shape[0], row_parts.shape[0]
    return pl.pallas_call(
        functools.partial(finish_kernel, factor, shift),
        out_shape=jax.ShapeDtypeStruct((rows, columns), jnp.bfloat16),
        grid=(ny,),
        in_specs=[
            pl.BlockSpec((rows, c), lambda j: (0, 0)),
            pl.BlockSpec((nx, 1, n, c), lambda j: (0, j, 0, 0)),
            pl.BlockSpec((nb, 1, rows), lambda j: (0, 0, 0)),
            pl.BlockSpec((na, 1, width), lambda j: (0, 0, j)),
            pl.BlockSpec((1, width), lambda j: (0, j)),
            pl.BlockSpec((1, width), lambda j: (0, j)),
        ],
        out_specs=pl.BlockSpec((rows, width), lambda j: (0, j)),
        scratch_shapes=[pltpu.VMEM((rows, 128), jnp.float32)],
        compiler_params=pltpu.CompilerParams(vmem_limit_bytes=40 << 20),
        name="confidence",
    )(a, b, row_parts, col_parts, col_max_other[None], col_sum_other[None])


def local(feat_a, feat_b, col_max_other, col_sum_other):
    factor = 1.0 / (feat_a.shape[1] * TEMPER)
    columns = feat_b.shape[0] * lax.axis_size(AA)
    shift = math.log2(float(FRAME_A) * float(columns * lax.axis_size(BA)))
    a = spread(feat_a, BA).reshape(-1, feat_a.shape[1])
    b = spread(spread(feat_b, "y"), "x")
    row_lse, col_lse = stats(a, b, factor)
    row_parts = spread(row_lse, BA)
    col_parts = spread(col_lse, AA)
    return finish(a, b, row_parts, col_parts, col_max_other, col_sum_other, factor, shift)


def solution(mesh):
    inner = Mesh(mesh.devices.reshape(8, 4, 8, 2), AA + BA)
    in_specs = (P(AA + BA, None), P(BA + AA, None), P(BA), P(BA))
    out_specs = P(AA, BA)
    return jax.shard_map(local, mesh=inner, in_specs=in_specs, out_specs=out_specs, check_vma=False)
```

time: 450 us -> 123 us (0.27)
  the two profiles are of different devices: /device:TPU:32 before, /device:TPU:1 now
where the time goes in v1:
time: 123 us
  blocking collectives  109 us (89%)
  Pallas kernels  11.6 us (9%)
  local copies, waits for them, and re-layouts  2.35 us (2%)
    all_to_all x5, blocking collectives, spread(): lax.all_to_all(jnp.broadcast_to(block[None], (n,) + block.shape), axis, 0...  109 us
    pallas_call x1, Pallas kernels, stats(): pl.pallas_call(functools.partial(stats_kernel, factor), out_shape=(jax.Sh...  6.05 us
    pallas_call x1, Pallas kernels, finish(): pl.pallas_call(functools.partial(finish_kernel, factor, shift), out_shape...  5.59 us

profile of v1, /device:TPU:1, one launch (start us, length us, event | category | flops | bytes accessed | tf_op | source)
XLA Modules:
  0.0 122.7 jit_solution(4997313728564574222)
XLA Ops:
  0.0 0.7 broadcast_in_dim.18
  0.7 23.3 %all_to_all.25 = bf16[16,32,256]{2,1,0:T(8,128)(2,1)S(1)} all-to-all(bf16[16,32,256]{2,1,0:T(8,128)(2,1)S(1)} %broadcast_in_dim.18), channel_id=1, replica_groups=mesh['y'=8,'x'=4,'z'=8,'core'=2] {'z','core'}, dimensions={0} | all-to-all | bytes 524288 | tf_op jit(solution)/shard_map/all_to_all | solution.py:21
  24.1 0.9 broadcast_in_dim.19
  25.0 24.6 %all_to_all.26 = bf16[8,128,256]{2,1,0:T(8,128)(2,1)S(1)} all-to-all(bf16[8,128,256]{2,1,0:T(8,128)(2,1)S(1)} %broadcast_in_dim.19), channel_id=1, replica_groups=mesh['y'=8,'x'=4,'z'=8,'core'=2] {'y'}, dimensions={0} | all-to-all | bytes 1048576 | tf_op jit(solution)/shard_map/all_to_all | solution.py:21
  49.6 0.2 broadcast_in_dim.20
  49.8 29.2 %all_to_all.27.b_ref = bf16[4,8,128,256]{3,2,1,0:T(8,128)(2,1)S(1)} all-to-all(bf16[4,8,128,256]{3,2,1,0:T(8,128)(2,1)S(1)} %broadcast_in_dim.20), channel_id=1, replica_groups=mesh['y'=8,'x'=4,'z'=8,'core'=2] {'x'}, dimensions={0} | all-to-all | bytes 4194304 | tf_op jit(solution)/shard_map/all_to_all | solution.py:21
  79.1 0.0 copy-start
  79.1 0.0 copy-start.1
  79.1 6.1 %tile_statistics.1 = (f32[1,512]{1,0:T(1,128)S(1)}, f32[1,4096]{1,0:T(1,128)S(1)}) custom-call(bf16[512,256]{1,0:T(8,128)(2,1)S(1)} %bitcast.5, bf16[4,8,128,256]{3,2,1,0:T(8,128)(2,1)S(1)} %all_to_all.27.b_ref), custom_call_target="tpu_custom_call" | custom-call | tf_op jit(solution)/shard_map/tile_statistics/pallas_call | solution.py:66
  85.2 11.7 %all_to_all.28.rows_ref = f32[16,1,512]{2,1,0:T(1,128)S(1)} all-to-all(f32[16,1,512]{2,1,0:T(1,128)S(1)} %broadcast_in_dim.44), channel_id=1, replica_groups=mesh['y'=8,'x'=4,'z'=8,'core'=2] {'z','core'}, dimensions={0} | all-to-all | bytes 65536 | tf_op jit(solution)/shard_map/all_to_all | solution.py:21
  96.9 0.5 broadcast_in_dim.46
  97.4 19.7 %all_to_all.29.cols_ref = f32[32,1,4096]{2,1,0:T(1,128)S(1)} all-to-all(f32[32,1,4096]{2,1,0:T(1,128)S(1)} %broadcast_in_dim.46), channel_id=1, replica_groups=mesh['y'=8,'x'=4,'z'=8,'core'=2] {'y','x'}, dimensions={0} | all-to-all | bytes 1048576 | tf_op jit(solution)/shard_map/all_to_all | solution.py:21
  117.1 0.0 copy-done
  117.1 0.0 copy-done.1
  117.1 5.6 %confidence.1 = bf16[512,4096]{1,0:T(8,128)(2,1)} custom-call(bf16[512,256]{1,0:T(8,128)(2,1)S(1)} %bitcast.6, bf16[4,8,128,256]{3,2,1,0:T(8,128)(2,1)S(1)} %all_to_all.27.b_ref, f32[16,1,512]{2,1,0:T(1,128)S(1)} %all_to_all.28.rows_ref, f32[32,1,4096]{2,1,0:T(1,128)S(1)} %all_to_all.29.cols_ref, f32[1,4096]{1,0:T(1,128)S(1)} %bitcast.7, f32[1,4096]{1,0:T(1,128)S(1)} %bitcast.8), custom_call_target="tpu_custom_call" | custom-call | tf_op jit(solution)/shard_map/confidence/pallas_call | solution.py:105
  (1 shorter events, 0.0 us)
Async XLA Ops:
  79.1 38.0 %copy-start = (f32[4096]{0:T(1024)S(1)}, f32[4096]{0:T(1024)}, u32[]{:S(2)}) copy-start(f32[4096]{0:T(1024)} %param.6) | copy-start | bytes 49156
  79.1 38.0 %copy-start.1 = (f32[4096]{0:T(1024)S(1)}, f32[4096]{0:T(1024)}, u32[]{:S(2)}) copy-start(f32[4096]{0:T(1024)} %param.7) | copy-start | bytes 49156

commit v2 on v0

v2 whole, which is shorter than its diff:
```python
import functools
import math

import jax
import jax.numpy as jnp
from jax import lax
from jax.experimental import pallas as pl
from jax.experimental.pallas import tpu as pltpu
from jax.sharding import Mesh
from jax.sharding import PartitionSpec as P

FRAME_A = 131072
TEMPER = 0.1
LOG2E = math.log2(math.e)
AA = ("y", "x")
BA = ("z", "core")
LANES = 128
WIDTH = 256
SAFE_LOW, SAFE_HIGH = 2.0**-40, 2.0**100
VMEM_LIMIT = 48 << 20


def spread(block, axis):
    n = lax.axis_size(axis)
    return lax.all_to_all(jnp.broadcast_to(block[None], (n,) + block.shape), axis, 0, 0, tiled=True)


def scores(a, b, scale):
    return lax.dot_general(a, b, (((1,), (1,)), ((), ())), preferred_element_type=jnp.float32) * scale


def to_lanes(column):
    return jnp.sum(column.T, axis=0, keepdims=True)


def lse_over(parts, axis):
    top = jnp.max(parts, axis=axis, keepdims=True)
    return jnp.squeeze(top + jnp.log2(jnp.sum(jnp.exp2(parts - top), axis=axis, keepdims=True)), axis)


def part_statistics(scale, a_ref, b_refs, row_ref, col_ref):
    rows = a_ref.shape[0]
    blocks, n, c = b_refs[0].shape
    per = WIDTH // n
    work = [(ref, i) for ref in b_refs for i in range(0, blocks, per)]

    def put_col(t, lse):
        for k in range(per):
            col_ref[pl.ds(t * per + k, 1), :] = lse[:, k * LANES : (k + 1) * LANES]

    def put_row(lse):
        for k in range(rows // LANES):
            row_ref[pl.ds(k, 1), :] = lse[:, k * LANES : (k + 1) * LANES]

    tot = jnp.zeros((rows, LANES), jnp.float32)
    for t, (ref, i) in enumerate(work):
        e = jnp.exp2(scores(a_ref[...], ref[i : i + per].reshape(WIDTH, c), scale))
        put_col(t, jnp.log2(jnp.sum(e, axis=0, keepdims=True)))
        for k in range(per):
            tot = tot + e[:, k * LANES : (k + 1) * LANES]
    row_tot = to_lanes(tot)
    put_row(jnp.log2(row_tot))
    in_range = (jnp.min(row_tot) > SAFE_LOW) & (jnp.max(row_tot) < SAFE_HIGH)

    @pl.when(jnp.logical_not(in_range))
    def _():
        top = jnp.full((rows, 1), -jnp.inf, jnp.float32)
        for t, (ref, i) in enumerate(work):
            s = scores(a_ref[...], ref[i : i + per].reshape(WIDTH, c), scale)
            col_top = jnp.max(s, axis=0, keepdims=True)
            put_col(t, col_top + jnp.log2(jnp.sum(jnp.exp2(s - col_top), axis=0, keepdims=True)))
            top = jnp.maximum(top, jnp.max(s, axis=1, keepdims=True))
        tot = jnp.zeros((rows, LANES), jnp.float32)
        for ref, i in work:
            e = jnp.exp2(scores(a_ref[...], ref[i : i + per].reshape(WIDTH, c), scale) - top)
            for k in range(per):
                tot = tot + e[:, k * LANES : (k + 1) * LANES]
        row_top = jnp.broadcast_to(top, (rows, LANES)).T[:1]
        put_row(row_top + jnp.log2(to_lanes(tot)))


def early_kernel(scale, a_ref, *refs):
    part_statistics(scale, a_ref, refs[:-2], *refs[-2:])


def early_statistics(a, parts, scale):
    rows = a.shape[0]
    blocks = sum(p.shape[0] for p in parts)
    vmem = pl.BlockSpec(memory_space=pltpu.VMEM)
    return pl.pallas_call(
        functools.partial(early_kernel, scale),
        out_shape=(
            jax.ShapeDtypeStruct((rows // LANES, LANES), jnp.float32),
            jax.ShapeDtypeStruct((blocks, LANES), jnp.float32),
        ),
        in_specs=[vmem] * (1 + len(parts)),
        out_specs=(vmem, vmem),
        compiler_params=pltpu.CompilerParams(vmem_limit_bytes=VMEM_LIMIT),
        name="part_statistics",
    )(a, *parts)


def home(shift):
    n = lax.axis_size("x")
    return lax.rem(lax.axis_index("x") + n - shift, n)


def last_kernel(scale, shifts, a_ref, b_ref, *refs):
    early, (row_ref, col_ref, row_part, col_part, cols) = refs[:-5], refs[-5:]
    part_statistics(scale, a_ref, [b_ref], row_part, col_part)
    row_parts = [r[...] for r in early[0::2]] + [row_part[...]]
    row_ref[...] = lse_over(jnp.stack(row_parts), 0)
    col_parts = jnp.concatenate([c[...] for c in early[1::2]] + [col_part[...]], axis=0)
    nx = len(shifts)
    blocks = b_ref.shape[0]
    for p, shift in enumerate(shifts):
        x = home(shift)
        for y in range(blocks):
            cols[pl.ds(y * nx + x, 1), :] = col_parts[p * blocks + y : p * blocks + y + 1]
    col_ref[...] = jnp.broadcast_to(cols[...][None], col_ref.shape)


def last_statistics(a, part, early, shifts, scale, copies):
    rows = a.shape[0]
    blocks = part.shape[0] * len(shifts)
    vmem = pl.BlockSpec(memory_space=pltpu.VMEM)
    flat = [leaf for pair in early for leaf in pair]
    return pl.pallas_call(
        functools.partial(last_kernel, scale, shifts),
        out_shape=(
            jax.ShapeDtypeStruct((rows // LANES, LANES), jnp.float32),
            jax.ShapeDtypeStruct((copies, blocks, LANES), jnp.float32),
        ),
        in_specs=[vmem] * (2 + len(flat)),
        out_specs=(vmem, vmem),
        scratch_shapes=[
            pltpu.VMEM((rows // LANES, LANES), jnp.float32),
            pltpu.VMEM((part.shape[0], LANES), jnp.float32),
            pltpu.VMEM((blocks, LANES), jnp.float32),
        ],
        compiler_params=pltpu.CompilerParams(vmem_limit_bytes=VMEM_LIMIT),
        name="tile_statistics",
    )(a, part, *flat)


def finish_kernel(scale, shift_up, shifts, a_ref, *refs):
    nx = len(shifts)
    b_refs = refs[:nx]
    rows_ref, cols_ref, top_ref, tot_ref, out_ref, row_lse, col_lse, held, sems = refs[nx:]
    rows = a_ref.shape[0]
    blocks, n, c = b_refs[0].shape
    width = nx * n

    lse = lse_over(rows_ref[...], 0)
    for k in range(rows // LANES):
        row_lse[pl.ds(k * LANES, LANES), :] = jnp.broadcast_to(lse[k : k + 1], (LANES, LANES)).T

    parts = cols_ref[...]
    other = top_ref[...] * LOG2E
    top = jnp.maximum(jnp.max(parts, axis=0), other)
    tot = jnp.sum(jnp.exp2(parts - top[None]), axis=0) + tot_ref[...] * jnp.exp2(other - top)
    col_lse[...] = top + jnp.log2(tot) - shift_up

    def copy(y):
        return pltpu.make_async_copy(held.at[y], out_ref.at[:, pl.ds(y * width, width)], sems.at[y])

    homes = [home(shift) for shift in shifts]
    per = WIDTH // n
    for y in range(blocks):
        for p in range(0, nx, per):
            b = jnp.concatenate([ref[y] for ref in b_refs[p : p + per]], axis=0)
            s = scores(a_ref[...], b, scale)
            for k in range(per):
                x = homes[p + k]
                part = s[:, k * n : (k + 1) * n]
                col = col_lse[pl.ds(y * nx + x, 1), :]
                e = jnp.exp2((part - row_lse[...]) + (part - col))
                held[y, :, pl.ds(pl.multiple_of(x * n, n), n)] = e.astype(held.dtype)
        copy(y).start()
    for y in range(blocks):
        copy(y).wait()


def finish(a, parts, row_parts, col_parts, col_max_other, col_sum_other, shifts, scale, shift_up):
    rows = a.shape[0]
    blocks, n, _ = parts[0].shape
    width = n * len(parts)
    vmem = pl.BlockSpec(memory_space=pltpu.VMEM)
    return pl.pallas_call(
        functools.partial(finish_kernel, scale, shift_up, shifts),
        out_shape=jax.ShapeDtypeStruct((rows, blocks * width), jnp.bfloat16),
        in_specs=[vmem] * (5 + len(parts)),
        out_specs=pl.BlockSpec(memory_space=pl.ANY),
        scratch_shapes=[
            pltpu.VMEM((rows, LANES), jnp.float32),
            pltpu.VMEM((blocks * len(parts), LANES), jnp.float32),
            pltpu.VMEM((blocks, rows, width), jnp.bfloat16),
            pltpu.SemaphoreType.DMA((blocks,)),
        ],
        compiler_params=pltpu.CompilerParams(vmem_limit_bytes=VMEM_LIMIT),
        name="confidence",
    )(a, *parts, row_parts, col_parts, col_max_other.reshape(-1, LANES), col_sum_other.reshape(-1, LANES))


def shifted(block, shift):
    n = lax.axis_size("x")
    return lax.ppermute(block, "x", [(i, (i + shift) % n) for i in range(n)])


def local(feat_a, feat_b, col_max_other, col_sum_other):
    scale = LOG2E / (feat_a.shape[1] * TEMPER)
    columns = feat_b.shape[0] * lax.axis_size(AA)
    shift_up = math.log2(float(FRAME_A) * float(columns * lax.axis_size(BA)))
    shifts = (0, 1, 3, 2)
    a = lax.all_gather(feat_a, BA, axis=0, tiled=True)
    own = spread(feat_b, "y")
    parts = [own] + [shifted(own, k) for k in shifts[1:]]
    early = [early_statistics(a, parts[:1], scale), early_statistics(a, parts[1:3], scale)]
    row_lse, col_copies = last_statistics(a, parts[3], early, shifts, scale, lax.axis_size(AA))
    row_parts = lax.all_gather(row_lse, BA, axis=0)
    col_parts = lax.all_to_all(col_copies, AA, 0, 0, tiled=True)
    return finish(a, parts, row_parts, col_parts, col_max_other, col_sum_other, shifts, scale, shift_up)


def solution(mesh):
    inner = Mesh(mesh.devices.reshape(8, 4, 8, 2), AA + BA)
    in_specs = (P(AA + BA, None), P(BA + AA, None), P(BA), P(BA))
    out_specs = P(AA, BA)
    return jax.shard_map(local, mesh=inner, in_specs=in_specs, out_specs=out_specs, check_vma=False)
```

time: 450 us -> 90.2 us (0.20)
  the two profiles are of different devices: /device:TPU:32 before, /device:TPU:1 now
where the time goes in v2:
time: 90.2 us; the launch traced here: 89.8 us
  blocking collectives  67.7 us (75%)
  starting transfers between devices  15.1 us (17%)
  Pallas kernels  6.11 us (7%)
    all_gather x1, blocking collectives, local(): a = lax.all_gather(feat_a, BA, axis=0, tiled=True)  27.2 us
    all_to_all x1, blocking collectives, spread(): lax.all_to_all(jnp.broadcast_to(block[None], (n,) + block.shape), axis, 0...  22.2 us
    all_gather x1, blocking collectives, local(): row_parts = lax.all_gather(row_lse, BA, axis=0)  18.2 us
    ppermute x3, starting transfers between devices, shifted(): return lax.ppermute(block, 'x', [(i, (i + shift) % n) for i in range(n)])  11.2 us
    all_to_all x1, starting transfers between devices, local(): col_parts = lax.all_to_all(col_copies, AA, 0, 0, tiled=True)  3.89 us
    pallas_call x1, Pallas kernels, finish(): pl.pallas_call(functools.partial(finish_kernel, scale, shift_up, shifts),...  2.89 us
  transfers between devices with their start and end apart: 4, of which 0 were waited for; matrix products, arithmetic and copies ran while one was open for 0% of the time, Pallas kernels for 2%

profile of v2, /device:TPU:1, one launch (start us, length us, event | category | flops | bytes accessed | tf_op | source)
XLA Modules:
  0.0 89.8 jit_solution(1986592776562027212)
XLA Ops:
  0.0 0.0 copy-start.1
  0.0 0.0 copy-start
  0.0 0.9 broadcast_in_dim.2
  0.9 22.2 %all_to_all.10.refs_0_ = bf16[8,128,256]{2,1,0:T(8,128)(2,1)S(1)} all-to-all(bf16[8,128,256]{2,1,0:T(8,128)(2,1)S(1)} %broadcast_in_dim.2), channel_id=1, replica_groups=mesh['y'=8,'x'=4,'z'=8,'core'=2] {'y'}, dimensions={0} | all-to-all | bytes 1048576 | tf_op jit(solution)/shard_map/all_to_all | solution.py:25
  23.1 5.6 %collective-permute-start.1 = (bf16[8,128,256]{2,1,0:T(8,128)(2,1)S(1)}, bf16[8,128,256]{2,1,0:T(8,128)(2,1)S(1)}, u32[]{:S(2)}, u32[]{:S(2)}) collective-permute-start(bf16[8,128,256]{2,1,0:T(8,128)(2,1)S(1)} %all_to_all.10.refs_0_), channel_id=1, source_target_pairs={{0,48},{16,0},{32,16},{48,32},{1,49},{17,1},{33,17},{49,33},{2,50}... | collective-permute-start | bytes 1572872 | tf_op jit(solution)/shard_map/ppermute | solution.py:207
  28.7 1.9 %collective-permute-start = (bf16[8,128,256]{2,1,0:T(8,128)(2,1)S(1)}, bf16[8,128,256]{2,1,0:T(8,128)(2,1)S(1)}, u32[]{:S(2)}, u32[]{:S(2)}) collective-permute-start(bf16[8,128,256]{2,1,0:T(8,128)(2,1)S(1)} %all_to_all.10.refs_0_), channel_id=1, source_target_pairs={{0,16},{16,32},{32,48},{48,0},{1,17},{17,33},{33,49},{49,1},{2,18}... | collective-permute-start | bytes 1572872 | tf_op jit(solution)/shard_map/ppermute | solution.py:207
  30.7 3.6 %collective-permute-start.2 = (bf16[8,128,256]{2,1,0:T(8,128)(2,1)S(1)}, bf16[8,128,256]{2,1,0:T(8,128)(2,1)S(1)}, u32[]{:S(2)}, u32[]{:S(2)}) collective-permute-start(bf16[8,128,256]{2,1,0:T(8,128)(2,1)S(1)} %all_to_all.10.refs_0_), channel_id=1, source_target_pairs={{0,32},{16,48},{32,0},{48,16},{1,33},{17,49},{33,1},{49,17},{2,34}... | collective-permute-start | bytes 1572872 | tf_op jit(solution)/shard_map/ppermute | solution.py:207
  34.3 27.2 %all_gather.9.a_ref = bf16[512,256]{1,0:T(8,128)(2,1)S(1)} all-gather(bf16[32,256]{1,0:T(8,128)(2,1)} %param.4), channel_id=1, replica_groups=mesh['y'=8,'x'=4,'z'=8,'core'=2] {'z','core'}, dimensions={0}, use_global_device_ids=true | all-gather | bytes 278528 | tf_op jit(solution)/shard_map/all_gather | solution.py:215
  61.5 0.7 part_statistics.2
  62.2 0.0 collective-permute-done.1.refs_1_.refs_2_
  62.2 0.0 collective-permute-done.refs_0_.refs_1_
  62.2 1.0 %part_statistics.3 = (f32[4,128]{1,0:T(4,128)S(1)}, f32[16,128]{1,0:T(8,128)S(1)}) custom-call(bf16[512,256]{1,0:T(8,128)(2,1)S(1)} %all_gather.9.a_ref, bf16[8,128,256]{2,1,0:T(8,128)(2,1)S(1)} %collective-permute-done.refs_0_.refs_1_, bf16[8,128,256]{2,1,0:T(8,128)(2,1)S(1)} %collective-permute-done.1.refs_1_.refs_2_), custom_call_target="tpu_custom_call" | custom-call | tf_op jit(solution)/shard_map/part_statistics/pallas_call | solution.py:90
  63.2 0.0 collective-permute-done.2.b_ref.refs_3_
  63.2 1.6 %tile_statistics.1 = (f32[4,128]{1,0:T(4,128)S(1)}, f32[32,32,128]{2,1,0:T(8,128)}) custom-call(bf16[512,256]{1,0:T(8,128)(2,1)S(1)} %all_gather.9.a_ref, bf16[8,128,256]{2,1,0:T(8,128)(2,1)S(1)} %collective-permute-done.2.b_ref.refs_3_, f32[4,128]{1,0:T(4,128)S(1)} %get-tuple-element.11.refs_0_, f32[8,128]{1,0:T(8,128)S(1)} %get-tuple-element.12.refs_1_, ...), custom_call_target="tpu_custom_call" | custom-call | tf_op jit(solution)/shard_map/tile_statistics/pallas_call | solution.py:128
  64.8 3.9 %all-to-all-start.1 = ((f32[32,32,128]{2,1,0:T(8,128)}), f32[32,32,128]{2,1,0:T(8,128)S(1)}, u32[]{:S(2)}, u32[]{:S(2)}) async-start(f32[32,32,128]{2,1,0:T(8,128)} %get-tuple-element.16), calls=%async_computation.1 | async-start | bytes 1048576 | tf_op jit(solution)/shard_map/all_to_all | solution.py:221
  68.7 18.2 %all-gather.1.refs_4_ = f32[16,4,128]{2,1,0:T(4,128)S(1)} all-gather(f32[1,4,128]{2,1,0:T(4,128)S(1)} %bitcast.5), channel_id=2, replica_groups=mesh['y'=8,'x'=4,'z'=8,'core'=2] {'z','core'}, dimensions={0}, use_global_device_ids=true | all-gather | bytes 34816 | tf_op jit(solution)/shard_map/all_gather | solution.py:220
  86.9 0.0 all-to-all-done.1.refs_5_
  86.9 0.0 copy-done.1
  86.9 0.0 copy-done
  86.9 2.9 %confidence.1 = bf16[512,4096]{1,0:T(8,128)(2,1)} custom-call(bf16[512,256]{1,0:T(8,128)(2,1)S(1)} %all_gather.9.a_ref, bf16[8,128,256]{2,1,0:T(8,128)(2,1)S(1)} %all_to_all.10.refs_0_, bf16[8,128,256]{2,1,0:T(8,128)(2,1)S(1)} %collective-permute-done.refs_0_.refs_1_, bf16[8,128,256]{2,1,0:T(8,128)(2,1)S(1)} %collective-permute-done.1.refs_1_.refs_2_, ...), custom_call_target="tpu_custom_call" | custom-call | tf_op jit(solution)/shard_map/confidence/pallas_call | solution.py:189
Async XLA Ops:
  0.0 86.9 %copy-start.1 = (f32[4096]{0:T(1024)S(1)}, f32[4096]{0:T(1024)}, u32[]{:S(2)}) copy-start(f32[4096]{0:T(1024)} %param.7) | copy-start | bytes 49156
  0.0 86.9 %copy-start = (f32[4096]{0:T(1024)S(1)}, f32[4096]{0:T(1024)}, u32[]{:S(2)}) copy-start(f32[4096]{0:T(1024)} %param.6) | copy-start | bytes 49156
  23.1 39.1 %collective-permute-start.1 = (bf16[8,128,256]{2,1,0:T(8,128)(2,1)S(1)}, bf16[8,128,256]{2,1,0:T(8,128)(2,1)S(1)}, u32[]{:S(2)}, u32[]{:S(2)}) collective-permute-start(bf16[8,128,256]{2,1,0:T(8,128)(2,1)S(1)} %all_to_all.10.refs_0_), channel_id=1, source_target_pairs={{0,48},{16,0},{32,16},{48,32},{1,49},{17,1},{33,17},{49,33},{2,50}... | collective-permute-start | bytes 1572872 | tf_op jit(solution)/shard_map/ppermute | solution.py:207
  28.7 33.5 %collective-permute-start = (bf16[8,128,256]{2,1,0:T(8,128)(2,1)S(1)}, bf16[8,128,256]{2,1,0:T(8,128)(2,1)S(1)}, u32[]{:S(2)}, u32[]{:S(2)}) collective-permute-start(bf16[8,128,256]{2,1,0:T(8,128)(2,1)S(1)} %all_to_all.10.refs_0_), channel_id=1, source_target_pairs={{0,16},{16,32},{32,48},{48,0},{1,17},{17,33},{33,49},{49,1},{2,18}... | collective-permute-start | bytes 1572872 | tf_op jit(solution)/shard_map/ppermute | solution.py:207
  30.7 32.6 %collective-permute-start.2 = (bf16[8,128,256]{2,1,0:T(8,128)(2,1)S(1)}, bf16[8,128,256]{2,1,0:T(8,128)(2,1)S(1)}, u32[]{:S(2)}, u32[]{:S(2)}) collective-permute-start(bf16[8,128,256]{2,1,0:T(8,128)(2,1)S(1)} %all_to_all.10.refs_0_), channel_id=1, source_target_pairs={{0,32},{16,48},{32,0},{48,16},{1,33},{17,49},{33,1},{49,17},{2,34}... | collective-permute-start | bytes 1572872 | tf_op jit(solution)/shard_map/ppermute | solution.py:207
  64.8 22.1 %all-to-all-start.1 = ((f32[32,32,128]{2,1,0:T(8,128)}), f32[32,32,128]{2,1,0:T(8,128)S(1)}, u32[]{:S(2)}, u32[]{:S(2)}) async-start(f32[32,32,128]{2,1,0:T(8,128)} %get-tuple-element.16), calls=%async_computation.1 | async-start | bytes 1048576 | tf_op jit(solution)/shard_map/all_to_all | solution.py:221

commit v3 on v2

--- a/solution.py
+++ b/solution.py
@@ -105,14 +105,14 @@
     return lax.rem(lax.axis_index("x") + n - shift, n)
 
 
-def last_kernel(scale, shifts, a_ref, b_ref, *refs):
-    early, (row_ref, col_ref, row_part, col_part, cols) = refs[:-5], refs[-5:]
-    part_statistics(scale, a_ref, [b_ref], row_part, col_part)
+def last_kernel(scale, shifts, count, a_ref, *refs):
+    b_refs, early, (row_ref, col_ref, row_part, col_part, cols) = refs[:count], refs[count:-5], refs[-5:]
+    part_statistics(scale, a_ref, b_refs, row_part, col_part)
     row_parts = [r[...] for r in early[0::2]] + [row_part[...]]
     row_ref[...] = lse_over(jnp.stack(row_parts), 0)
     col_parts = jnp.concatenate([c[...] for c in early[1::2]] + [col_part[...]], axis=0)
     nx = len(shifts)
-    blocks = b_ref.shape[0]
+    blocks = b_refs[0].shape[0]
     for p, shift in enumerate(shifts):
         x = home(shift)
         for y in range(blocks):
@@ -120,27 +120,28 @@
     col_ref[...] = jnp.broadcast_to(cols[...][None], col_ref.shape)
 
 
-def last_statistics(a, part, early, shifts, scale, copies):
+def last_statistics(a, parts, early, shifts, scale, copies):
     rows = a.shape[0]
-    blocks = part.shape[0] * len(shifts)
+    last = parts[0].shape[0] * len(parts)
+    blocks = parts[0].shape[0] * len(shifts)
     vmem = pl.BlockSpec(memory_space=pltpu.VMEM)
     flat = [leaf for pair in early for leaf in pair]
     return pl.pallas_call(
-        functools.partial(last_kernel, scale, shifts),
+        functools.partial(last_kernel, scale, shifts, len(parts)),
         out_shape=(
             jax.ShapeDtypeStruct((rows // LANES, LANES), jnp.float32),
             jax.ShapeDtypeStruct((copies, blocks, LANES), jnp.float32),
         ),
-        in_specs=[vmem] * (2 + len(flat)),
+        in_specs=[vmem] * (1 + len(parts) + len(flat)),
         out_specs=(vmem, vmem),
         scratch_shapes=[
             pltpu.VMEM((rows // LANES, LANES), jnp.float32),
-            pltpu.VMEM((part.shape[0], LANES), jnp.float32),
+            pltpu.VMEM((last, LANES), jnp.float32),
             pltpu.VMEM((blocks, LANES), jnp.float32),
         ],
         compiler_params=pltpu.CompilerParams(vmem_limit_bytes=VMEM_LIMIT),
         name="tile_statistics",
-    )(a, part, *flat)
+    )(a, *parts, *flat)
 
 
 def finish_kernel(scale, shift_up, shifts, a_ref, *refs):
@@ -211,12 +212,13 @@
     scale = LOG2E / (feat_a.shape[1] * TEMPER)
     columns = feat_b.shape[0] * lax.axis_size(AA)
     shift_up = math.log2(float(FRAME_A) * float(columns * lax.axis_size(BA)))
-    shifts = (0, 1, 3, 2)
-    a = lax.all_gather(feat_a, BA, axis=0, tiled=True)
+    shifts = (0, 2, 1, 3)
     own = spread(feat_b, "y")
+    feat_a, own = lax.optimization_barrier((feat_a, own))
+    a = spread(feat_a, BA).reshape(-1, feat_a.shape[1])
     parts = [own] + [shifted(own, k) for k in shifts[1:]]
-    early = [early_statistics(a, parts[:1], scale), early_statistics(a, parts[1:3], scale)]
-    row_lse, col_copies = last_statistics(a, parts[3], early, shifts, scale, lax.axis_size(AA))
+    early = [early_statistics(a, parts[:1], scale), early_statistics(a, parts[1:2], scale)]
+    row_lse, col_copies = last_statistics(a, parts[2:], early, shifts, scale, lax.axis_size(AA))
     row_parts = lax.all_gather(row_lse, BA, axis=0)
     col_parts = lax.all_to_all(col_copies, AA, 0, 0, tiled=True)
     return finish(a, parts, row_parts, col_parts, col_max_other, col_sum_other, shifts, scale, shift_up)

time: 90.2 us -> 87.6 us (0.971)
  blocking collectives: 67.7 us -> 64 us
    all_gather x1 -> x0, blocking collectives: 27.2 us -> none  [local(): a = lax.all_gather(feat_a, BA, axis=0, tiled=True)]
    all_to_all x1 -> x2, blocking collectives: 22.2 us -> 47.3 us  [spread(): lax.all_to_all(jnp.broadcast_to(block[None], (n,) + block.shape), axis, 0...]
    all_gather x1, blocking collectives: 18.2 us -> 16.7 us  [local(): row_parts = lax.all_gather(row_lse, BA, axis=0)]
  transfers between devices with their start and end apart: 4 -> 4, of which waited for: 0 -> 0; matrix products, arithmetic and copies ran while one was open for 0% -> 1% of each run, Pallas kernels for 2% -> 2%
where the time goes in v3:
time: 87.6 us; the launch traced here: 86.9 us
  blocking collectives  64 us (73%)
  starting transfers between devices  15.1 us (17%)
  Pallas kernels  6.1 us (7%)
  local copies, waits for them, and re-layouts  1.63 us (2%)
    all_to_all x2, blocking collectives, spread(): lax.all_to_all(jnp.broadcast_to(block[None], (n,) + block.shape), axis, 0...  47.3 us
    all_gather x1, blocking collectives, local(): row_parts = lax.all_gather(row_lse, BA, axis=0)  16.7 us
    ppermute x3, starting transfers between devices, shifted(): return lax.ppermute(block, 'x', [(i, (i + shift) % n) for i in range(n)])  11.2 us
    all_to_all x1, starting transfers between devices, local(): col_parts = lax.all_to_all(col_copies, AA, 0, 0, tiled=True)  3.89 us
    pallas_call x1, Pallas kernels, finish(): pl.pallas_call(functools.partial(finish_kernel, scale, shift_up, shifts),...  2.88 us
    pallas_call x1, Pallas kernels, last_statistics(): pl.pallas_call(functools.partial(last_kernel, scale, shifts, len(parts)),...  1.86 us
  transfers between devices with their start and end apart: 4, of which 0 were waited for; matrix products, arithmetic and copies ran while one was open for 1% of the time, Pallas kernels for 2%

profile of v3, /device:TPU:1, one launch (start us, length us, event | category | flops | bytes accessed | tf_op | source)
XLA Modules:
  0.0 86.9 jit_solution(6640968385859136941)
XLA Ops:
  0.0 0.0 copy-start.1
  0.0 0.0 copy-start
  0.0 0.9 %broadcast_in_dim.4 = bf16[8,128,256]{2,1,0:T(8,128)(2,1)S(1)} broadcast(bf16[128,256]{1,0:T(8,128)(2,1)} %param.5), dimensions={1,2} | broadcast | bytes 589824 | tf_op jit(solution)/shard_map/broadcast_in_dim | solution.py:25
  0.9 22.2 %all_to_all.15.refs_0_ = bf16[8,128,256]{2,1,0:T(8,128)(2,1)S(1)} all-to-all(bf16[8,128,256]{2,1,0:T(8,128)(2,1)S(1)} %broadcast_in_dim.4), channel_id=1, replica_groups=mesh['y'=8,'x'=4,'z'=8,'core'=2] {'y'}, dimensions={0} | all-to-all | bytes 1048576 | tf_op jit(solution)/shard_map/all_to_all | solution.py:25
  23.1 5.9 %collective-permute-start = (bf16[8,128,256]{2,1,0:T(8,128)(2,1)S(1)}, bf16[8,128,256]{2,1,0:T(8,128)(2,1)S(1)}, u32[]{:S(2)}, u32[]{:S(2)}) collective-permute-start(bf16[8,128,256]{2,1,0:T(8,128)(2,1)S(1)} %all_to_all.15.refs_0_), channel_id=1, source_target_pairs={{0,32},{16,48},{32,0},{48,16},{1,33},{17,49},{33,1},{49,17},{2,34}... | collective-permute-start | bytes 1572872 | tf_op jit(solution)/shard_map/ppermute | solution.py:208
  29.0 2.8 %collective-permute-start.2 = (bf16[8,128,256]{2,1,0:T(8,128)(2,1)S(1)}, bf16[8,128,256]{2,1,0:T(8,128)(2,1)S(1)}, u32[]{:S(2)}, u32[]{:S(2)}) collective-permute-start(bf16[8,128,256]{2,1,0:T(8,128)(2,1)S(1)} %all_to_all.15.refs_0_), channel_id=1, source_target_pairs={{0,48},{16,0},{32,16},{48,32},{1,49},{17,1},{33,17},{49,33},{2,50}... | collective-permute-start | bytes 1572872 | tf_op jit(solution)/shard_map/ppermute | solution.py:208
  31.8 2.5 %collective-permute-start.1 = (bf16[8,128,256]{2,1,0:T(8,128)(2,1)S(1)}, bf16[8,128,256]{2,1,0:T(8,128)(2,1)S(1)}, u32[]{:S(2)}, u32[]{:S(2)}) collective-permute-start(bf16[8,128,256]{2,1,0:T(8,128)(2,1)S(1)} %all_to_all.15.refs_0_), channel_id=1, source_target_pairs={{0,16},{16,32},{32,48},{48,0},{1,17},{17,33},{33,49},{49,1},{2,18}... | collective-permute-start | bytes 1572872 | tf_op jit(solution)/shard_map/ppermute | solution.py:208
  34.3 0.7 broadcast_in_dim.5
  35.0 25.1 %all_to_all.16 = bf16[16,32,256]{2,1,0:T(8,128)(2,1)S(1)} all-to-all(bf16[16,32,256]{2,1,0:T(8,128)(2,1)S(1)} %broadcast_in_dim.5), channel_id=1, replica_groups=mesh['y'=8,'x'=4,'z'=8,'core'=2] {'z','core'}, dimensions={0} | all-to-all | bytes 524288 | tf_op jit(solution)/shard_map/all_to_all | solution.py:25
  60.2 0.7 part_statistics.2
  60.8 0.0 collective-permute-done.refs_0_.refs_1_
  60.9 0.7 part_statistics.3
  61.5 0.0 collective-permute-done.2.refs_1_.refs_3_
  61.5 0.0 collective-permute-done.1.refs_0_.refs_2_
  61.6 1.9 %tile_statistics.1 = (f32[4,128]{1,0:T(4,128)S(1)}, f32[32,32,128]{2,1,0:T(8,128)}) custom-call(bf16[512,256]{1,0:T(8,128)(2,1)S(1)} %bitcast.6, bf16[8,128,256]{2,1,0:T(8,128)(2,1)S(1)} %collective-permute-done.1.refs_0_.refs_2_, bf16[8,128,256]{2,1,0:T(8,128)(2,1)S(1)} %collective-permute-done.2.refs_1_.refs_3_, f32[4,128]{1,0:T(4,128)S(1)} %get-tuple-element.15.refs_2_, ...), custom_call_target="tpu_custom_call" | custom-call | tf_op jit(solution)/shard_map/tile_statistics/pallas_call | solution.py:129
  63.4 3.9 %all-to-all-start.2 = ((f32[32,32,128]{2,1,0:T(8,128)}), f32[32,32,128]{2,1,0:T(8,128)S(1)}, u32[]{:S(2)}, u32[]{:S(2)}) async-start(f32[32,32,128]{2,1,0:T(8,128)} %get-tuple-element.20), calls=%async_computation.2 | async-start | bytes 1048576 | tf_op jit(solution)/shard_map/all_to_all | solution.py:223
  67.3 16.7 %all-gather.1.refs_4_ = f32[16,4,128]{2,1,0:T(4,128)S(1)} all-gather(f32[1,4,128]{2,1,0:T(4,128)S(1)} %bitcast.10), channel_id=2, replica_groups=mesh['y'=8,'x'=4,'z'=8,'core'=2] {'z','core'}, dimensions={0}, use_global_device_ids=true | all-gather | bytes 34816 | tf_op jit(solution)/shard_map/all_gather | solution.py:222
  84.0 0.0 all-to-all-done.2.refs_5_
  84.0 0.0 copy-done.1
  84.0 0.0 copy-done
  84.0 2.9 %confidence.1 = bf16[512,4096]{1,0:T(8,128)(2,1)} custom-call(bf16[512,256]{1,0:T(8,128)(2,1)S(1)} %bitcast.7, bf16[8,128,256]{2,1,0:T(8,128)(2,1)S(1)} %all_to_all.15.refs_0_, bf16[8,128,256]{2,1,0:T(8,128)(2,1)S(1)} %collective-permute-done.refs_0_.refs_1_, bf16[8,128,256]{2,1,0:T(8,128)(2,1)S(1)} %collective-permute-done.1.refs_0_.refs_2_, ...), custom_call_target="tpu_custom_call" | custom-call | tf_op jit(solution)/shard_map/confidence/pallas_call | solution.py:190
Async XLA Ops:
  0.0 84.0 %copy-start.1 = (f32[4096]{0:T(1024)S(1)}, f32[4096]{0:T(1024)}, u32[]{:S(2)}) copy-start(f32[4096]{0:T(1024)} %param.7) | copy-start | bytes 49156
  0.0 84.0 %copy-start = (f32[4096]{0:T(1024)S(1)}, f32[4096]{0:T(1024)}, u32[]{:S(2)}) copy-start(f32[4096]{0:T(1024)} %param.6) | copy-start | bytes 49156
  23.1 37.8 %collective-permute-start = (bf16[8,128,256]{2,1,0:T(8,128)(2,1)S(1)}, bf16[8,128,256]{2,1,0:T(8,128)(2,1)S(1)}, u32[]{:S(2)}, u32[]{:S(2)}) collective-permute-start(bf16[8,128,256]{2,1,0:T(8,128)(2,1)S(1)} %all_to_all.15.refs_0_), channel_id=1, source_target_pairs={{0,32},{16,48},{32,0},{48,16},{1,33},{17,49},{33,1},{49,17},{2,34}... | collective-permute-start | bytes 1572872 | tf_op jit(solution)/shard_map/ppermute | solution.py:208
  29.0 32.6 %collective-permute-start.2 = (bf16[8,128,256]{2,1,0:T(8,128)(2,1)S(1)}, bf16[8,128,256]{2,1,0:T(8,128)(2,1)S(1)}, u32[]{:S(2)}, u32[]{:S(2)}) collective-permute-start(bf16[8,128,256]{2,1,0:T(8,128)(2,1)S(1)} %all_to_all.15.refs_0_), channel_id=1, source_target_pairs={{0,48},{16,0},{32,16},{48,32},{1,49},{17,1},{33,17},{49,33},{2,50}... | collective-permute-start | bytes 1572872 | tf_op jit(solution)/shard_map/ppermute | solution.py:208
  31.8 29.8 %collective-permute-start.1 = (bf16[8,128,256]{2,1,0:T(8,128)(2,1)S(1)}, bf16[8,128,256]{2,1,0:T(8,128)(2,1)S(1)}, u32[]{:S(2)}, u32[]{:S(2)}) collective-permute-start(bf16[8,128,256]{2,1,0:T(8,128)(2,1)S(1)} %all_to_all.15.refs_0_), channel_id=1, source_target_pairs={{0,16},{16,32},{32,48},{48,0},{1,17},{17,33},{33,49},{49,1},{2,18}... | collective-permute-start | bytes 1572872 | tf_op jit(solution)/shard_map/ppermute | solution.py:208
  63.4 20.6 %all-to-all-start.2 = ((f32[32,32,128]{2,1,0:T(8,128)}), f32[32,32,128]{2,1,0:T(8,128)S(1)}, u32[]{:S(2)}, u32[]{:S(2)}) async-start(f32[32,32,128]{2,1,0:T(8,128)} %get-tuple-element.20), calls=%async_computation.2 | async-start | bytes 1048576 | tf_op jit(solution)/shard_map/all_to_all | solution.py:223

commit v4 on v3

--- a/solution.py
+++ b/solution.py
@@ -65,16 +65,25 @@
     @pl.when(jnp.logical_not(in_range))
     def _():
         top = jnp.full((rows, 1), -jnp.inf, jnp.float32)
-        for t, (ref, i) in enumerate(work):
-            s = scores(a_ref[...], ref[i : i + per].reshape(WIDTH, c), scale)
-            col_top = jnp.max(s, axis=0, keepdims=True)
-            put_col(t, col_top + jnp.log2(jnp.sum(jnp.exp2(s - col_top), axis=0, keepdims=True)))
-            top = jnp.maximum(top, jnp.max(s, axis=1, keepdims=True))
         tot = jnp.zeros((rows, LANES), jnp.float32)
-        for ref, i in work:
-            e = jnp.exp2(scores(a_ref[...], ref[i : i + per].reshape(WIDTH, c), scale) - top)
-            for k in range(per):
-                tot = tot + e[:, k * LANES : (k + 1) * LANES]
+        for q, ref in enumerate(b_refs):
+
+            def first(i, top, q=q, ref=ref):
+                s = scores(a_ref[...], ref[pl.ds(i * per, per)].reshape(WIDTH, c), scale)
+                col_top = jnp.max(s, axis=0, keepdims=True)
+                put_col(q * (blocks // per) + i, col_top + jnp.log2(jnp.sum(jnp.exp2(s - col_top), axis=0, keepdims=True)))
+                return jnp.maximum(top, jnp.max(s, axis=1, keepdims=True))
+
+            top = lax.fori_loop(0, blocks // per, first, top)
+        for ref in b_refs:
+
+            def second(i, tot, ref=ref):
+                e = jnp.exp2(scores(a_ref[...], ref[pl.ds(i * per, per)].reshape(WIDTH, c), scale) - top)
+                for k in range(per):
+                    tot = tot + e[:, k * LANES : (k + 1) * LANES]
+                return tot
+
+            tot = lax.fori_loop(0, blocks // per, second, tot)
         row_top = jnp.broadcast_to(top, (rows, LANES)).T[:1]
         put_row(row_top + jnp.log2(to_lanes(tot)))
 
@@ -217,10 +226,10 @@
     feat_a, own = lax.optimization_barrier((feat_a, own))
     a = spread(feat_a, BA).reshape(-1, feat_a.shape[1])
     parts = [own] + [shifted(own, k) for k in shifts[1:]]
-    early = [early_statistics(a, parts[:1], scale), early_statistics(a, parts[1:2], scale)]
+    early = [early_statistics(a, parts[:2], scale)]
     row_lse, col_copies = last_statistics(a, parts[2:], early, shifts, scale, lax.axis_size(AA))
     row_parts = lax.all_gather(row_lse, BA, axis=0)
-    col_parts = lax.all_to_all(col_copies, AA, 0, 0, tiled=True)
+    col_parts = lax.all_to_all(col_copies, AA[::-1], 0, 0, tiled=True)
     return finish(a, parts, row_parts, col_parts, col_max_other, col_sum_other, shifts, scale, shift_up)
 
 

time: 87.6 us -> 89.8 us (1.025)
  blocking collectives: 64 us -> 66.8 us
    all_gather x1, blocking collectives: 16.7 us -> 19.5 us  [local(): row_parts = lax.all_gather(row_lse, BA, axis=0)]
  transfers between devices with their start and end apart: 4 -> 4, of which waited for: 0 -> 0; matrix products, arithmetic and copies ran while one was open for 1% -> 1% of each run, Pallas kernels for 2% -> 1%
where the time goes in v4:
time: 89.8 us; the launch traced here: 89.3 us
  blocking collectives  66.8 us (74%)
  starting transfers between devices  15.1 us (17%)
  Pallas kernels  5.73 us (6%)
  local copies, waits for them, and re-layouts  1.63 us (2%)
    all_to_all x2, blocking collectives, spread(): lax.all_to_all(jnp.broadcast_to(block[None], (n,) + block.shape), axis, 0...  47.3 us
    all_gather x1, blocking collectives, local(): row_parts = lax.all_gather(row_lse, BA, axis=0)  19.5 us
    ppermute x3, starting transfers between devices, shifted(): return lax.ppermute(block, 'x', [(i, (i + shift) % n) for i in range(n)])  11.2 us
    all_to_all x1, starting transfers between devices, local(): col_parts = lax.all_to_all(col_copies, AA[::-1], 0, 0, tiled=True)  3.89 us
    pallas_call x1, Pallas kernels, finish(): pl.pallas_call(functools.partial(finish_kernel, scale, shift_up, shifts),...  2.88 us
    pallas_call x1, Pallas kernels, last_statistics(): pl.pallas_call(functools.partial(last_kernel, scale, shifts, len(parts)),...  1.86 us
  transfers between devices with their start and end apart: 4, of which 0 were waited for; matrix products, arithmetic and copies ran while one was open for 1% of the time, Pallas kernels for 1%

profile of v4, /device:TPU:1, one launch (start us, length us, event | category | flops | bytes accessed | tf_op | source)
XLA Modules:
  0.0 89.3 jit_solution(7659224944817603829)
XLA Ops:
  0.0 0.0 copy-start.1
  0.0 0.0 copy-start
  0.0 0.9 broadcast_in_dim.4
  0.9 22.2 %all_to_all.15.refs_0_ = bf16[8,128,256]{2,1,0:T(8,128)(2,1)S(1)} all-to-all(bf16[8,128,256]{2,1,0:T(8,128)(2,1)S(1)} %broadcast_in_dim.4), channel_id=1, replica_groups=mesh['y'=8,'x'=4,'z'=8,'core'=2] {'y'}, dimensions={0} | all-to-all | bytes 1048576 | tf_op jit(solution)/shard_map/all_to_all | solution.py:25
  23.1 5.9 %collective-permute-start = (bf16[8,128,256]{2,1,0:T(8,128)(2,1)S(1)}, bf16[8,128,256]{2,1,0:T(8,128)(2,1)S(1)}, u32[]{:S(2)}, u32[]{:S(2)}) collective-permute-start(bf16[8,128,256]{2,1,0:T(8,128)(2,1)S(1)} %all_to_all.15.refs_0_), channel_id=1, source_target_pairs={{0,32},{16,48},{32,0},{48,16},{1,33},{17,49},{33,1},{49,17},{2,34}... | collective-permute-start | bytes 1572872 | tf_op jit(solution)/shard_map/ppermute | solution.py:217
  29.0 2.8 %collective-permute-start.2 = (bf16[8,128,256]{2,1,0:T(8,128)(2,1)S(1)}, bf16[8,128,256]{2,1,0:T(8,128)(2,1)S(1)}, u32[]{:S(2)}, u32[]{:S(2)}) collective-permute-start(bf16[8,128,256]{2,1,0:T(8,128)(2,1)S(1)} %all_to_all.15.refs_0_), channel_id=1, source_target_pairs={{0,48},{16,0},{32,16},{48,32},{1,49},{17,1},{33,17},{49,33},{2,50}... | collective-permute-start | bytes 1572872 | tf_op jit(solution)/shard_map/ppermute | solution.py:217
  31.8 2.5 %collective-permute-start.1 = (bf16[8,128,256]{2,1,0:T(8,128)(2,1)S(1)}, bf16[8,128,256]{2,1,0:T(8,128)(2,1)S(1)}, u32[]{:S(2)}, u32[]{:S(2)}) collective-permute-start(bf16[8,128,256]{2,1,0:T(8,128)(2,1)S(1)} %all_to_all.15.refs_0_), channel_id=1, source_target_pairs={{0,16},{16,32},{32,48},{48,0},{1,17},{17,33},{33,49},{49,1},{2,18}... | collective-permute-start | bytes 1572872 | tf_op jit(solution)/shard_map/ppermute | solution.py:217
  34.3 0.7 broadcast_in_dim.5
  35.0 25.1 %all_to_all.16 = bf16[16,32,256]{2,1,0:T(8,128)(2,1)S(1)} all-to-all(bf16[16,32,256]{2,1,0:T(8,128)(2,1)S(1)} %broadcast_in_dim.5), channel_id=1, replica_groups=mesh['y'=8,'x'=4,'z'=8,'core'=2] {'z','core'}, dimensions={0} | all-to-all | bytes 524288 | tf_op jit(solution)/shard_map/all_to_all | solution.py:25
  60.2 0.0 collective-permute-done.refs_1_
  60.2 1.0 %part_statistics.1 = (f32[4,128]{1,0:T(4,128)S(1)}, f32[16,128]{1,0:T(8,128)S(1)}) custom-call(bf16[512,256]{1,0:T(8,128)(2,1)S(1)} %bitcast.4, bf16[8,128,256]{2,1,0:T(8,128)(2,1)S(1)} %all_to_all.15.refs_0_, bf16[8,128,256]{2,1,0:T(8,128)(2,1)S(1)} %collective-permute-done.refs_1_), custom_call_target="tpu_custom_call" | custom-call | tf_op jit(solution)/shard_map/part_statistics/pallas_call | solution.py:99
  61.2 0.0 collective-permute-done.2.refs_1_.refs_3_
  61.2 0.0 collective-permute-done.1.refs_0_.refs_2_
  61.2 1.9 %tile_statistics.1 = (f32[4,128]{1,0:T(4,128)S(1)}, f32[32,32,128]{2,1,0:T(8,128)}) custom-call(bf16[512,256]{1,0:T(8,128)(2,1)S(1)} %bitcast.5, bf16[8,128,256]{2,1,0:T(8,128)(2,1)S(1)} %collective-permute-done.1.refs_0_.refs_2_, bf16[8,128,256]{2,1,0:T(8,128)(2,1)S(1)} %collective-permute-done.2.refs_1_.refs_3_, f32[4,128]{1,0:T(4,128)S(1)} %get-tuple-element.13.refs_2_, ...), custom_call_target="tpu_custom_call" | custom-call | tf_op jit(solution)/shard_map/tile_statistics/pallas_call | solution.py:138
  63.0 3.9 %all-to-all-start.2 = ((f32[32,32,128]{2,1,0:T(8,128)}), f32[32,32,128]{2,1,0:T(8,128)S(1)}, u32[]{:S(2)}, u32[]{:S(2)}) async-start(f32[32,32,128]{2,1,0:T(8,128)} %get-tuple-element.16), calls=%async_computation.2 | async-start | bytes 1048576 | tf_op jit(solution)/shard_map/all_to_all | solution.py:232
  66.9 19.5 %all-gather.1.refs_4_ = f32[16,4,128]{2,1,0:T(4,128)S(1)} all-gather(f32[1,4,128]{2,1,0:T(4,128)S(1)} %bitcast.9), channel_id=2, replica_groups=mesh['y'=8,'x'=4,'z'=8,'core'=2] {'z','core'}, dimensions={0}, use_global_device_ids=true | all-gather | bytes 34816 | tf_op jit(solution)/shard_map/all_gather | solution.py:231
  86.4 0.0 all-to-all-done.2.refs_5_
  86.4 0.0 copy-done.1
  86.4 0.0 copy-done
  86.4 2.9 %confidence.1 = bf16[512,4096]{1,0:T(8,128)(2,1)} custom-call(bf16[512,256]{1,0:T(8,128)(2,1)S(1)} %bitcast.6, bf16[8,128,256]{2,1,0:T(8,128)(2,1)S(1)} %all_to_all.15.refs_0_, bf16[8,128,256]{2,1,0:T(8,128)(2,1)S(1)} %collective-permute-done.refs_1_, bf16[8,128,256]{2,1,0:T(8,128)(2,1)S(1)} %collective-permute-done.1.refs_0_.refs_2_, ...), custom_call_target="tpu_custom_call" | custom-call | tf_op jit(solution)/shard_map/confidence/pallas_call | solution.py:199
Async XLA Ops:
  0.0 86.4 %copy-start.1 = (f32[4096]{0:T(1024)S(1)}, f32[4096]{0:T(1024)}, u32[]{:S(2)}) copy-start(f32[4096]{0:T(1024)} %param.7) | copy-start | bytes 49156
  0.0 86.4 %copy-start = (f32[4096]{0:T(1024)S(1)}, f32[4096]{0:T(1024)}, u32[]{:S(2)}) copy-start(f32[4096]{0:T(1024)} %param.6) | copy-start | bytes 49156
  23.1 37.1 %collective-permute-start = (bf16[8,128,256]{2,1,0:T(8,128)(2,1)S(1)}, bf16[8,128,256]{2,1,0:T(8,128)(2,1)S(1)}, u32[]{:S(2)}, u32[]{:S(2)}) collective-permute-start(bf16[8,128,256]{2,1,0:T(8,128)(2,1)S(1)} %all_to_all.15.refs_0_), channel_id=1, source_target_pairs={{0,32},{16,48},{32,0},{48,16},{1,33},{17,49},{33,1},{49,17},{2,34}... | collective-permute-start | bytes 1572872 | tf_op jit(solution)/shard_map/ppermute | solution.py:217
  29.0 32.2 %collective-permute-start.2 = (bf16[8,128,256]{2,1,0:T(8,128)(2,1)S(1)}, bf16[8,128,256]{2,1,0:T(8,128)(2,1)S(1)}, u32[]{:S(2)}, u32[]{:S(2)}) collective-permute-start(bf16[8,128,256]{2,1,0:T(8,128)(2,1)S(1)} %all_to_all.15.refs_0_), channel_id=1, source_target_pairs={{0,48},{16,0},{32,16},{48,32},{1,49},{17,1},{33,17},{49,33},{2,50}... | collective-permute-start | bytes 1572872 | tf_op jit(solution)/shard_map/ppermute | solution.py:217
  31.8 29.4 %collective-permute-start.1 = (bf16[8,128,256]{2,1,0:T(8,128)(2,1)S(1)}, bf16[8,128,256]{2,1,0:T(8,128)(2,1)S(1)}, u32[]{:S(2)}, u32[]{:S(2)}) collective-permute-start(bf16[8,128,256]{2,1,0:T(8,128)(2,1)S(1)} %all_to_all.15.refs_0_), channel_id=1, source_target_pairs={{0,16},{16,32},{32,48},{48,0},{1,17},{17,33},{33,49},{49,1},{2,18}... | collective-permute-start | bytes 1572872 | tf_op jit(solution)/shard_map/ppermute | solution.py:217
  63.0 23.4 %all-to-all-start.2 = ((f32[32,32,128]{2,1,0:T(8,128)}), f32[32,32,128]{2,1,0:T(8,128)S(1)}, u32[]{:S(2)}, u32[]{:S(2)}) async-start(f32[32,32,128]{2,1,0:T(8,128)} %get-tuple-element.16), calls=%async_computation.2 | async-start | bytes 1048576 | tf_op jit(solution)/shard_map/all_to_all | solution.py:232

commit v5 on v4

--- a/solution.py
+++ b/solution.py
@@ -15,14 +15,16 @@
 AA = ("y", "x")
 BA = ("z", "core")
 LANES = 128
+Y_ORDER = (3, 4, 2, 5, 1, 6, 0, 7)
 WIDTH = 256
 SAFE_LOW, SAFE_HIGH = 2.0**-40, 2.0**100
 VMEM_LIMIT = 48 << 20
 
 
-def spread(block, axis):
+def spread(block, axis, order=None):
     n = lax.axis_size(axis)
-    return lax.all_to_all(jnp.broadcast_to(block[None], (n,) + block.shape), axis, 0, 0, tiled=True)
+    copies = jnp.broadcast_to(block[None], (n,) + block.shape)
+    return lax.all_to_all(copies, axis, 0, 0, tiled=True, axis_index_groups=None if order is None else [list(order)])
 
 
 def scores(a, b, scale):
@@ -124,8 +126,8 @@
     blocks = b_refs[0].shape[0]
     for p, shift in enumerate(shifts):
         x = home(shift)
-        for y in range(blocks):
-            cols[pl.ds(y * nx + x, 1), :] = col_parts[p * blocks + y : p * blocks + y + 1]
+        for i, y in enumerate(Y_ORDER):
+            cols[pl.ds(y * nx + x, 1), :] = col_parts[p * blocks + i : p * blocks + i + 1]
     col_ref[...] = jnp.broadcast_to(cols[...][None], col_ref.shape)
 
 
@@ -176,9 +178,9 @@
 
     homes = [home(shift) for shift in shifts]
     per = WIDTH // n
-    for y in range(blocks):
+    for i, y in enumerate(Y_ORDER):
         for p in range(0, nx, per):
-            b = jnp.concatenate([ref[y] for ref in b_refs[p : p + per]], axis=0)
+            b = jnp.concatenate([ref[i] for ref in b_refs[p : p + per]], axis=0)
             s = scores(a_ref[...], b, scale)
             for k in range(per):
                 x = homes[p + k]
@@ -222,7 +224,7 @@
     columns = feat_b.shape[0] * lax.axis_size(AA)
     shift_up = math.log2(float(FRAME_A) * float(columns * lax.axis_size(BA)))
     shifts = (0, 2, 1, 3)
-    own = spread(feat_b, "y")
+    own = spread(feat_b, "y", Y_ORDER)
     feat_a, own = lax.optimization_barrier((feat_a, own))
     a = spread(feat_a, BA).reshape(-1, feat_a.shape[1])
     parts = [own] + [shifted(own, k) for k in shifts[1:]]

time: 89.8 us -> 87.6 us (0.976)
  blocking collectives: 66.8 us -> 61 us
  starting transfers between devices: 15.1 us -> 18.6 us
    all_to_all x2, blocking collectives: 47.3 us -> 43.3 us  [spread(): lax.all_to_all(copies, axis, 0, 0, tiled=True, axis_index_groups=None if...]
    all_to_all x1, starting transfers between devices: 3.89 us -> 6.07 us  [local(): col_parts = lax.all_to_all(col_copies, AA[::-1], 0, 0, tiled=True)]
    all_gather x1, blocking collectives: 19.5 us -> 17.7 us  [local(): row_parts = lax.all_gather(row_lse, BA, axis=0)]
    ppermute x3, starting transfers between devices: 11.2 us -> 12.5 us  [shifted(): return lax.ppermute(block, 'x', [(i, (i + shift) % n) for i in range(n)])]
where the time goes in v5:
time: 87.6 us; the launch traced here: 87.1 us
  blocking collectives  61 us (70%)
  starting transfers between devices  18.6 us (21%)
  Pallas kernels  5.74 us (7%)
  local copies, waits for them, and re-layouts  1.63 us (2%)
    all_to_all x2, blocking collectives, spread(): lax.all_to_all(copies, axis, 0, 0, tiled=True, axis_index_groups=None if...  43.3 us
    all_gather x1, blocking collectives, local(): row_parts = lax.all_gather(row_lse, BA, axis=0)  17.7 us
    ppermute x3, starting transfers between devices, shifted(): return lax.ppermute(block, 'x', [(i, (i + shift) % n) for i in range(n)])  12.5 us
    all_to_all x1, starting transfers between devices, local(): col_parts = lax.all_to_all(col_copies, AA[::-1], 0, 0, tiled=True)  6.07 us
    pallas_call x1, Pallas kernels, finish(): pl.pallas_call(functools.partial(finish_kernel, scale, shift_up, shifts),...  2.91 us
    pallas_call x1, Pallas kernels, last_statistics(): pl.pallas_call(functools.partial(last_kernel, scale, shifts, len(parts)),...  1.85 us
  transfers between devices with their start and end apart: 4, of which 0 were waited for; matrix products, arithmetic and copies ran while one was open for 1% of the time, Pallas kernels for 1%

profile of v5, /device:TPU:1, one launch (start us, length us, event | category | flops | bytes accessed | tf_op | source)
XLA Modules:
  0.0 87.1 jit_solution(1933007941993624323)
XLA Ops:
  0.0 0.0 copy-start.1
  0.0 0.0 copy-start
  0.0 0.9 %broadcast_in_dim.4 = bf16[8,128,256]{2,1,0:T(8,128)(2,1)S(1)} broadcast(bf16[128,256]{1,0:T(8,128)(2,1)} %param.5), dimensions={1,2} | broadcast | bytes 589824 | tf_op jit(solution)/shard_map/broadcast_in_dim | solution.py:26
  0.9 19.2 %all_to_all.15.refs_0_ = bf16[8,128,256]{2,1,0:T(8,128)(2,1)S(1)} all-to-all(bf16[8,128,256]{2,1,0:T(8,128)(2,1)S(1)} %broadcast_in_dim.4), channel_id=1, replica_groups={{192,256,128,320,64,384,0,448},{193,257,129,321,65,385,1,449},{194,258,..., dimensions={0} | all-to-all | bytes 1048576 | tf_op jit(solution)/shard_map/all_to_all | solution.py:27
  20.1 7.3 %collective-permute-start = (bf16[8,128,256]{2,1,0:T(8,128)(2,1)S(1)}, bf16[8,128,256]{2,1,0:T(8,128)(2,1)S(1)}, u32[]{:S(2)}, u32[]{:S(2)}) collective-permute-start(bf16[8,128,256]{2,1,0:T(8,128)(2,1)S(1)} %all_to_all.15.refs_0_), channel_id=1, source_target_pairs={{0,32},{16,48},{32,0},{48,16},{1,33},{17,49},{33,1},{49,17},{2,34}... | collective-permute-start | bytes 1572872 | tf_op jit(solution)/shard_map/ppermute | solution.py:219
  27.4 2.8 %collective-permute-start.2 = (bf16[8,128,256]{2,1,0:T(8,128)(2,1)S(1)}, bf16[8,128,256]{2,1,0:T(8,128)(2,1)S(1)}, u32[]{:S(2)}, u32[]{:S(2)}) collective-permute-start(bf16[8,128,256]{2,1,0:T(8,128)(2,1)S(1)} %all_to_all.15.refs_0_), channel_id=1, source_target_pairs={{0,48},{16,0},{32,16},{48,32},{1,49},{17,1},{33,17},{49,33},{2,50}... | collective-permute-start | bytes 1572872 | tf_op jit(solution)/shard_map/ppermute | solution.py:219
  30.1 2.5 %collective-permute-start.1 = (bf16[8,128,256]{2,1,0:T(8,128)(2,1)S(1)}, bf16[8,128,256]{2,1,0:T(8,128)(2,1)S(1)}, u32[]{:S(2)}, u32[]{:S(2)}) collective-permute-start(bf16[8,128,256]{2,1,0:T(8,128)(2,1)S(1)} %all_to_all.15.refs_0_), channel_id=1, source_target_pairs={{0,16},{16,32},{32,48},{48,0},{1,17},{17,33},{33,49},{49,1},{2,18}... | collective-permute-start | bytes 1572872 | tf_op jit(solution)/shard_map/ppermute | solution.py:219
  32.7 0.7 broadcast_in_dim.5
  33.4 24.1 %all_to_all.16 = bf16[16,32,256]{2,1,0:T(8,128)(2,1)S(1)} all-to-all(bf16[16,32,256]{2,1,0:T(8,128)(2,1)S(1)} %broadcast_in_dim.5), channel_id=1, replica_groups=mesh['y'=8,'x'=4,'z'=8,'core'=2] {'z','core'}, dimensions={0} | all-to-all | bytes 524288 | tf_op jit(solution)/shard_map/all_to_all | solution.py:27
  57.5 0.0 collective-permute-done.refs_1_
  57.5 1.0 %part_statistics.1 = (f32[4,128]{1,0:T(4,128)S(1)}, f32[16,128]{1,0:T(8,128)S(1)}) custom-call(bf16[512,256]{1,0:T(8,128)(2,1)S(1)} %bitcast.4, bf16[8,128,256]{2,1,0:T(8,128)(2,1)S(1)} %all_to_all.15.refs_0_, bf16[8,128,256]{2,1,0:T(8,128)(2,1)S(1)} %collective-permute-done.refs_1_), custom_call_target="tpu_custom_call" | custom-call | tf_op jit(solution)/shard_map/part_statistics/pallas_call | solution.py:101
  58.5 0.0 collective-permute-done.2.refs_1_.refs_3_
  58.5 0.0 collective-permute-done.1.refs_0_.refs_2_
  58.5 1.8 %tile_statistics.1 = (f32[4,128]{1,0:T(4,128)S(1)}, f32[32,32,128]{2,1,0:T(8,128)}) custom-call(bf16[512,256]{1,0:T(8,128)(2,1)S(1)} %bitcast.5, bf16[8,128,256]{2,1,0:T(8,128)(2,1)S(1)} %collective-permute-done.1.refs_0_.refs_2_, bf16[8,128,256]{2,1,0:T(8,128)(2,1)S(1)} %collective-permute-done.2.refs_1_.refs_3_, f32[4,128]{1,0:T(4,128)S(1)} %get-tuple-element.13.refs_2_, ...), custom_call_target="tpu_custom_call" | custom-call | tf_op jit(solution)/shard_map/tile_statistics/pallas_call | solution.py:140
  60.3 6.1 %all-to-all-start.2 = ((f32[32,32,128]{2,1,0:T(8,128)}), f32[32,32,128]{2,1,0:T(8,128)S(1)}, u32[]{:S(2)}, u32[]{:S(2)}) async-start(f32[32,32,128]{2,1,0:T(8,128)} %get-tuple-element.16), calls=%async_computation.2 | async-start | bytes 1048576 | tf_op jit(solution)/shard_map/all_to_all | solution.py:234
  66.4 17.7 %all-gather.1.refs_4_ = f32[16,4,128]{2,1,0:T(4,128)S(1)} all-gather(f32[1,4,128]{2,1,0:T(4,128)S(1)} %bitcast.9), channel_id=2, replica_groups=mesh['y'=8,'x'=4,'z'=8,'core'=2] {'z','core'}, dimensions={0}, use_global_device_ids=true | all-gather | bytes 34816 | tf_op jit(solution)/shard_map/all_gather | solution.py:233
  84.1 0.0 all-to-all-done.2.refs_5_
  84.1 0.0 copy-done.1
  84.1 0.0 copy-done
  84.2 2.9 %confidence.1 = bf16[512,4096]{1,0:T(8,128)(2,1)} custom-call(bf16[512,256]{1,0:T(8,128)(2,1)S(1)} %bitcast.6, bf16[8,128,256]{2,1,0:T(8,128)(2,1)S(1)} %all_to_all.15.refs_0_, bf16[8,128,256]{2,1,0:T(8,128)(2,1)S(1)} %collective-permute-done.refs_1_, bf16[8,128,256]{2,1,0:T(8,128)(2,1)S(1)} %collective-permute-done.1.refs_0_.refs_2_, ...), custom_call_target="tpu_custom_call" | custom-call | tf_op jit(solution)/shard_map/confidence/pallas_call | solution.py:201
Async XLA Ops:
  0.0 84.1 %copy-start.1 = (f32[4096]{0:T(1024)S(1)}, f32[4096]{0:T(1024)}, u32[]{:S(2)}) copy-start(f32[4096]{0:T(1024)} %param.7) | copy-start | bytes 49156
  0.0 84.1 %copy-start = (f32[4096]{0:T(1024)S(1)}, f32[4096]{0:T(1024)}, u32[]{:S(2)}) copy-start(f32[4096]{0:T(1024)} %param.6) | copy-start | bytes 49156
  20.1 37.4 %collective-permute-start = (bf16[8,128,256]{2,1,0:T(8,128)(2,1)S(1)}, bf16[8,128,256]{2,1,0:T(8,128)(2,1)S(1)}, u32[]{:S(2)}, u32[]{:S(2)}) collective-permute-start(bf16[8,128,256]{2,1,0:T(8,128)(2,1)S(1)} %all_to_all.15.refs_0_), channel_id=1, source_target_pairs={{0,32},{16,48},{32,0},{48,16},{1,33},{17,49},{33,1},{49,17},{2,34}... | collective-permute-start | bytes 1572872 | tf_op jit(solution)/shard_map/ppermute | solution.py:219
  27.4 31.1 %collective-permute-start.2 = (bf16[8,128,256]{2,1,0:T(8,128)(2,1)S(1)}, bf16[8,128,256]{2,1,0:T(8,128)(2,1)S(1)}, u32[]{:S(2)}, u32[]{:S(2)}) collective-permute-start(bf16[8,128,256]{2,1,0:T(8,128)(2,1)S(1)} %all_to_all.15.refs_0_), channel_id=1, source_target_pairs={{0,48},{16,0},{32,16},{48,32},{1,49},{17,1},{33,17},{49,33},{2,50}... | collective-permute-start | bytes 1572872 | tf_op jit(solution)/shard_map/ppermute | solution.py:219
  30.1 28.3 %collective-permute-start.1 = (bf16[8,128,256]{2,1,0:T(8,128)(2,1)S(1)}, bf16[8,128,256]{2,1,0:T(8,128)(2,1)S(1)}, u32[]{:S(2)}, u32[]{:S(2)}) collective-permute-start(bf16[8,128,256]{2,1,0:T(8,128)(2,1)S(1)} %all_to_all.15.refs_0_), channel_id=1, source_target_pairs={{0,16},{16,32},{32,48},{48,0},{1,17},{17,33},{33,49},{49,1},{2,18}... | collective-permute-start | bytes 1572872 | tf_op jit(solution)/shard_map/ppermute | solution.py:219
  60.3 23.8 %all-to-all-start.2 = ((f32[32,32,128]{2,1,0:T(8,128)}), f32[32,32,128]{2,1,0:T(8,128)S(1)}, u32[]{:S(2)}, u32[]{:S(2)}) async-start(f32[32,32,128]{2,1,0:T(8,128)} %get-tuple-element.16), calls=%async_computation.2 | async-start | bytes 1048576 | tf_op jit(solution)/shard_map/all_to_all | solution.py:234

commit v6 on v5

--- a/solution.py
+++ b/solution.py
@@ -181,12 +181,12 @@
     for i, y in enumerate(Y_ORDER):
         for p in range(0, nx, per):
             b = jnp.concatenate([ref[i] for ref in b_refs[p : p + per]], axis=0)
-            s = scores(a_ref[...], b, scale)
+            s = scores(a_ref[...], b, 2.0 * scale)
             for k in range(per):
                 x = homes[p + k]
                 part = s[:, k * n : (k + 1) * n]
                 col = col_lse[pl.ds(y * nx + x, 1), :]
-                e = jnp.exp2((part - row_lse[...]) + (part - col))
+                e = jnp.exp2((part - row_lse[...]) - col)
                 held[y, :, pl.ds(pl.multiple_of(x * n, n), n)] = e.astype(held.dtype)
         copy(y).start()
     for y in range(blocks):

time: 87.6 us -> 87.4 us (level)
  no operation moved by 1% of the time
where the time goes in v6:
time: 87.4 us; the launch traced here: 86.9 us
  blocking collectives  61 us (70%)
  starting transfers between devices  18.6 us (21%)
  Pallas kernels  5.54 us (6%)
  local copies, waits for them, and re-layouts  1.63 us (2%)
    all_to_all x2, blocking collectives, spread(): lax.all_to_all(copies, axis, 0, 0, tiled=True, axis_index_groups=None if...  43.3 us
    all_gather x1, blocking collectives, local(): row_parts = lax.all_gather(row_lse, BA, axis=0)  17.7 us
    ppermute x3, starting transfers between devices, shifted(): return lax.ppermute(block, 'x', [(i, (i + shift) % n) for i in range(n)])  12.5 us
    all_to_all x1, starting transfers between devices, local(): col_parts = lax.all_to_all(col_copies, AA[::-1], 0, 0, tiled=True)  6.07 us
    pallas_call x1, Pallas kernels, finish(): pl.pallas_call(functools.partial(finish_kernel, scale, shift_up, shifts),...  2.71 us
    pallas_call x1, Pallas kernels, last_statistics(): pl.pallas_call(functools.partial(last_kernel, scale, shifts, len(parts)),...  1.85 us
  transfers between devices with their start and end apart: 4, of which 0 were waited for; matrix products, arithmetic and copies ran while one was open for 1% of the time, Pallas kernels for 1%

profile of v6, /device:TPU:1, one launch (start us, length us, event | category | flops | bytes accessed | tf_op | source)
XLA Modules:
  0.0 86.9 jit_solution(4006405997406796051)
XLA Ops:
  0.0 0.0 copy-start.1
  0.0 0.0 copy-start
  0.0 0.9 %broadcast_in_dim.4 = bf16[8,128,256]{2,1,0:T(8,128)(2,1)S(1)} broadcast(bf16[128,256]{1,0:T(8,128)(2,1)} %param.5), dimensions={1,2} | broadcast | bytes 589824 | tf_op jit(solution)/shard_map/broadcast_in_dim | solution.py:26
  0.9 19.2 %all_to_all.15.refs_0_ = bf16[8,128,256]{2,1,0:T(8,128)(2,1)S(1)} all-to-all(bf16[8,128,256]{2,1,0:T(8,128)(2,1)S(1)} %broadcast_in_dim.4), channel_id=1, replica_groups={{192,256,128,320,64,384,0,448},{193,257,129,321,65,385,1,449},{194,258,..., dimensions={0} | all-to-all | bytes 1048576 | tf_op jit(solution)/shard_map/all_to_all | solution.py:27
  20.1 7.3 %collective-permute-start = (bf16[8,128,256]{2,1,0:T(8,128)(2,1)S(1)}, bf16[8,128,256]{2,1,0:T(8,128)(2,1)S(1)}, u32[]{:S(2)}, u32[]{:S(2)}) collective-permute-start(bf16[8,128,256]{2,1,0:T(8,128)(2,1)S(1)} %all_to_all.15.refs_0_), channel_id=1, source_target_pairs={{0,32},{16,48},{32,0},{48,16},{1,33},{17,49},{33,1},{49,17},{2,34}... | collective-permute-start | bytes 1572872 | tf_op jit(solution)/shard_map/ppermute | solution.py:219
  27.4 2.8 %collective-permute-start.2 = (bf16[8,128,256]{2,1,0:T(8,128)(2,1)S(1)}, bf16[8,128,256]{2,1,0:T(8,128)(2,1)S(1)}, u32[]{:S(2)}, u32[]{:S(2)}) collective-permute-start(bf16[8,128,256]{2,1,0:T(8,128)(2,1)S(1)} %all_to_all.15.refs_0_), channel_id=1, source_target_pairs={{0,48},{16,0},{32,16},{48,32},{1,49},{17,1},{33,17},{49,33},{2,50}... | collective-permute-start | bytes 1572872 | tf_op jit(solution)/shard_map/ppermute | solution.py:219
  30.1 2.5 %collective-permute-start.1 = (bf16[8,128,256]{2,1,0:T(8,128)(2,1)S(1)}, bf16[8,128,256]{2,1,0:T(8,128)(2,1)S(1)}, u32[]{:S(2)}, u32[]{:S(2)}) collective-permute-start(bf16[8,128,256]{2,1,0:T(8,128)(2,1)S(1)} %all_to_all.15.refs_0_), channel_id=1, source_target_pairs={{0,16},{16,32},{32,48},{48,0},{1,17},{17,33},{33,49},{49,1},{2,18}... | collective-permute-start | bytes 1572872 | tf_op jit(solution)/shard_map/ppermute | solution.py:219
  32.7 0.7 broadcast_in_dim.5
  33.4 24.1 %all_to_all.16 = bf16[16,32,256]{2,1,0:T(8,128)(2,1)S(1)} all-to-all(bf16[16,32,256]{2,1,0:T(8,128)(2,1)S(1)} %broadcast_in_dim.5), channel_id=1, replica_groups=mesh['y'=8,'x'=4,'z'=8,'core'=2] {'z','core'}, dimensions={0} | all-to-all | bytes 524288 | tf_op jit(solution)/shard_map/all_to_all | solution.py:27
  57.5 0.0 collective-permute-done.refs_1_
  57.5 1.0 %part_statistics.1 = (f32[4,128]{1,0:T(4,128)S(1)}, f32[16,128]{1,0:T(8,128)S(1)}) custom-call(bf16[512,256]{1,0:T(8,128)(2,1)S(1)} %bitcast.4, bf16[8,128,256]{2,1,0:T(8,128)(2,1)S(1)} %all_to_all.15.refs_0_, bf16[8,128,256]{2,1,0:T(8,128)(2,1)S(1)} %collective-permute-done.refs_1_), custom_call_target="tpu_custom_call" | custom-call | tf_op jit(solution)/shard_map/part_statistics/pallas_call | solution.py:101
  58.5 0.0 collective-permute-done.2.refs_1_.refs_3_
  58.5 0.0 collective-permute-done.1.refs_0_.refs_2_
  58.5 1.8 %tile_statistics.1 = (f32[4,128]{1,0:T(4,128)S(1)}, f32[32,32,128]{2,1,0:T(8,128)}) custom-call(bf16[512,256]{1,0:T(8,128)(2,1)S(1)} %bitcast.5, bf16[8,128,256]{2,1,0:T(8,128)(2,1)S(1)} %collective-permute-done.1.refs_0_.refs_2_, bf16[8,128,256]{2,1,0:T(8,128)(2,1)S(1)} %collective-permute-done.2.refs_1_.refs_3_, f32[4,128]{1,0:T(4,128)S(1)} %get-tuple-element.13.refs_2_, ...), custom_call_target="tpu_custom_call" | custom-call | tf_op jit(solution)/shard_map/tile_statistics/pallas_call | solution.py:140
  60.3 6.1 %all-to-all-start.2 = ((f32[32,32,128]{2,1,0:T(8,128)}), f32[32,32,128]{2,1,0:T(8,128)S(1)}, u32[]{:S(2)}, u32[]{:S(2)}) async-start(f32[32,32,128]{2,1,0:T(8,128)} %get-tuple-element.16), calls=%async_computation.2 | async-start | bytes 1048576 | tf_op jit(solution)/shard_map/all_to_all | solution.py:234
  66.4 17.7 %all-gather.1.refs_4_ = f32[16,4,128]{2,1,0:T(4,128)S(1)} all-gather(f32[1,4,128]{2,1,0:T(4,128)S(1)} %bitcast.9), channel_id=2, replica_groups=mesh['y'=8,'x'=4,'z'=8,'core'=2] {'z','core'}, dimensions={0}, use_global_device_ids=true | all-gather | bytes 34816 | tf_op jit(solution)/shard_map/all_gather | solution.py:233
  84.1 0.0 all-to-all-done.2.refs_5_
  84.1 0.0 copy-done.1
  84.1 0.0 copy-done
  84.2 2.7 %confidence.1 = bf16[512,4096]{1,0:T(8,128)(2,1)} custom-call(bf16[512,256]{1,0:T(8,128)(2,1)S(1)} %bitcast.6, bf16[8,128,256]{2,1,0:T(8,128)(2,1)S(1)} %all_to_all.15.refs_0_, bf16[8,128,256]{2,1,0:T(8,128)(2,1)S(1)} %collective-permute-done.refs_1_, bf16[8,128,256]{2,1,0:T(8,128)(2,1)S(1)} %collective-permute-done.1.refs_0_.refs_2_, ...), custom_call_target="tpu_custom_call" | custom-call | tf_op jit(solution)/shard_map/confidence/pallas_call | solution.py:201
Async XLA Ops:
  0.0 84.1 %copy-start.1 = (f32[4096]{0:T(1024)S(1)}, f32[4096]{0:T(1024)}, u32[]{:S(2)}) copy-start(f32[4096]{0:T(1024)} %param.7) | copy-start | bytes 49156
  0.0 84.1 %copy-start = (f32[4096]{0:T(1024)S(1)}, f32[4096]{0:T(1024)}, u32[]{:S(2)}) copy-start(f32[4096]{0:T(1024)} %param.6) | copy-start | bytes 49156
  20.1 37.4 %collective-permute-start = (bf16[8,128,256]{2,1,0:T(8,128)(2,1)S(1)}, bf16[8,128,256]{2,1,0:T(8,128)(2,1)S(1)}, u32[]{:S(2)}, u32[]{:S(2)}) collective-permute-start(bf16[8,128,256]{2,1,0:T(8,128)(2,1)S(1)} %all_to_all.15.refs_0_), channel_id=1, source_target_pairs={{0,32},{16,48},{32,0},{48,16},{1,33},{17,49},{33,1},{49,17},{2,34}... | collective-permute-start | bytes 1572872 | tf_op jit(solution)/shard_map/ppermute | solution.py:219
  27.4 31.1 %collective-permute-start.2 = (bf16[8,128,256]{2,1,0:T(8,128)(2,1)S(1)}, bf16[8,128,256]{2,1,0:T(8,128)(2,1)S(1)}, u32[]{:S(2)}, u32[]{:S(2)}) collective-permute-start(bf16[8,128,256]{2,1,0:T(8,128)(2,1)S(1)} %all_to_all.15.refs_0_), channel_id=1, source_target_pairs={{0,48},{16,0},{32,16},{48,32},{1,49},{17,1},{33,17},{49,33},{2,50}... | collective-permute-start | bytes 1572872 | tf_op jit(solution)/shard_map/ppermute | solution.py:219
  30.1 28.3 %collective-permute-start.1 = (bf16[8,128,256]{2,1,0:T(8,128)(2,1)S(1)}, bf16[8,128,256]{2,1,0:T(8,128)(2,1)S(1)}, u32[]{:S(2)}, u32[]{:S(2)}) collective-permute-start(bf16[8,128,256]{2,1,0:T(8,128)(2,1)S(1)} %all_to_all.15.refs_0_), channel_id=1, source_target_pairs={{0,16},{16,32},{32,48},{48,0},{1,17},{17,33},{33,49},{49,1},{2,18}... | collective-permute-start | bytes 1572872 | tf_op jit(solution)/shard_map/ppermute | solution.py:219
  60.3 23.8 %all-to-all-start.2 = ((f32[32,32,128]{2,1,0:T(8,128)}), f32[32,32,128]{2,1,0:T(8,128)S(1)}, u32[]{:S(2)}, u32[]{:S(2)}) async-start(f32[32,32,128]{2,1,0:T(8,128)} %get-tuple-element.16), calls=%async_computation.2 | async-start | bytes 1048576 | tf_op jit(solution)/shard_map/all_to_all | solution.py:234
